TPU v7x, 128 devices: a whole 4x4x4 slice. The times are simulated.
128 devices in a mesh: dp: 8 (over z_lo, y), row: 8 (over x, z_hi), col: 2 (over core).
Axes of the slice: x: 4, y: 4, z: 4 (z_hi: 2, z_lo: 2; z = z_hi * 2 + z_lo), core: 2. Of those that a mesh axis runs over, the one named last changes fastest.
Arguments:
- block_in: bfloat16 [16, 1024, 1088], P('dp', 'row', 'col'), may hold values from -6 to 6
- query_key_value_weight: bfloat16 [3, 1088, 1088], P(None, 'row', 'col'), may hold values from -0.1875 to 0.1875
- bias_qv: float32 [2, 1088], P(None, 'row'), may hold values from -3 to 3
- output_weight: bfloat16 [1088, 1088], P('row', 'col'), may hold values from -1.5 to 1.5
- bias_out: float32 [1088], P('col'), may hold values from -3 to 3
- gain_one: float32 [1088], P('col'), may hold values from 0.5 to 1.5
- shift_one: float32 [1088], P('col'), may hold values from -2 to 2
- gain_two: float32 [1088], P('col'), may hold values from 0.5 to 1.5
- shift_two: float32 [1088], P('col'), may hold values from -2 to 2
- up_weight: bfloat16 [4352, 1088], P('row', 'col'), may hold values from -0.1875 to 0.1875
- bias_up: float32 [4352], P('row'), may hold values from -3 to 3
- down_weight: bfloat16 [4352, 1088], P('row', 'col'), may hold values from -0.09375 to 0.09375
- bias_down: float32 [1088], P('col'), may hold values from -3 to 3
- out_grad: bfloat16 [16, 1024, 1088], P('dp', 'row', 'col'), may hold values from -6 to 6
Outputs:
- block_out: bfloat16 [16, 1024, 1088], P('dp', 'row', 'col')
- in_grad: float32 [16, 1024, 1088], P('dp', 'row', 'col')
- grad_qkv: float32 [3, 1088, 1088], P(None, 'row', 'col')
- grad_bias_qv: float32 [2, 1088], P(None, 'row')
- grad_out: float32 [1088, 1088], P('row', 'col')
- grad_bias_out: float32 [1088], P('col')
- grad_gain_one: float32 [1088], P('col')
- grad_shift_one: float32 [1088], P('col')
- grad_gain_two: float32 [1088], P('col')
- grad_shift_two: float32 [1088], P('col')
- up_weight_gradient: float32 [4352, 1088], P('row', 'col')
- grad_bias_up: float32 [4352], P('row')
- down_weight_gradient: float32 [4352, 1088], P('row', 'col')
- grad_bias_down: float32 [1088], P('col')
All inputs are finite; a program needn't handle non-finite values.
Results may differ from a plain program's by a relative error of at most 0.012.
Values may be sent and summed in bfloat16 or wider, within the bound.
A program may use at most 192 MiB of HBM per device.

v0:
```python
import jax
import jax.numpy as jnp
from jax import lax
from jax.sharding import Mesh
from jax.sharding import PartitionSpec as P

HDIM = 64
ROW = ("row_0", "row_1")
DP_ROW = ("dp", "row_0", "row_1")


EPSILON = 1e-05
MASKED = -1e30


def gathered_total(x, axis):
    return lax.all_gather(x, axis).sum(0)


def sent_to_all(x, axis):
    size = lax.axis_size(axis)
    return lax.all_to_all(jnp.broadcast_to(x[None], (size, *x.shape)), axis, 0, 0, tiled=True)


def joined_along(parts, dim):
    parts = jnp.moveaxis(parts, 0, dim)
    lengths = parts.shape
    return parts.reshape(*lengths[:dim], lengths[dim] * lengths[dim + 1], *lengths[dim + 2 :])


def collect(x, axis, dim):
    parts = sent_to_all(x, axis)
    return joined_along(parts, dim)


def in_blocks(x, dim, size):
    lengths = x.shape
    parts = x.reshape(*lengths[:dim], size, lengths[dim] // size, *lengths[dim + 1 :])
    return jnp.moveaxis(parts, dim, 0)


def sum_at_owner(x, axis, dim):
    parts = in_blocks(x, dim, lax.axis_size(axis))
    arrived = lax.all_to_all(parts, axis, split_axis=0, concat_axis=0, tiled=True)
    return arrived.sum(axis=0)


def scatter_axes(x, axes, dim):
    if not axes:
        return x
    nearer = lax.psum_scatter(x, axes[0], scatter_dimension=dim, tiled=True)
    return scatter_axes(nearer, axes[1:], dim)


def taken_together(x, axis):
    return sent_to_all(x, axis).sum(axis=0)


def in_one(arrays, axis):
    vector, at, finished = (jnp.concatenate([a.reshape(-1) for a in arrays]), 0, [])
    subtotal = taken_together(vector, axis)
    for a in arrays:
        finished.append(subtotal[at : at + a.size].reshape(a.shape))
        at += a.size
    return tuple(finished)


def column_sums(first, second):
    return (gathered_total(first, "col"), gathered_total(second, "col"))


def gather_rows(values):
    return collect(values, ROW, 1)


def gather_columns(values):
    return collect(values, "col", 0)


def summed_column_block(values):
    return sum_at_owner(values, "col", 0)


def summed_row_block(values):
    return scatter_axes(values, ROW, 1)


def to_heads(values):
    return lax.all_to_all(values, ROW, split_axis=1, concat_axis=3, tiled=True)


def from_heads(values):
    return lax.all_to_all(values, ROW, split_axis=3, concat_axis=1, tiled=True)


def spread_queries(projected):
    return to_heads(projected[:, :, 0:1])


def collect_keys(projected):
    return lax.all_gather(projected[:, :, 1:3], ROW, axis=3, tiled=True)


def norm_forward(values, gain, shift):
    width = values.shape[2] * lax.axis_size("col")
    totals, squares = column_sums(jnp.sum(values, axis=2), jnp.sum(values * values, axis=2))
    centre = (totals / width)[..., None]
    inverse = lax.rsqrt((squares / width)[..., None] - centre * centre + EPSILON)
    centred = (values - centre) * inverse
    return (centred * gain + shift, centred, inverse)


def norm_backward(upstream, centred, inverse, gain):
    width = upstream.shape[2] * lax.axis_size("col")
    scaled = upstream * gain
    totals, crossed = column_sums(jnp.sum(scaled, axis=2), jnp.sum(scaled * centred, axis=2))
    result = inverse * (
        scaled - (totals / width)[..., None] - centred * (crossed / width)[..., None]
    )
    return (result, jnp.sum(upstream * centred, axis=(0, 1)), jnp.sum(upstream, axis=(0, 1)))


def gelu_slope(values):
    cumulative = 0.5 * (1.0 + lax.erf(values * 0.7071067811865476))
    density = jnp.exp(-0.5 * values * values) * 0.3989422804014327
    return cumulative + values * density


def head_slice(values, head, axis_dim):
    return lax.dynamic_slice_in_dim(values, head * HDIM, HDIM, axis_dim)


def per_device(
    block_in,
    query_key_value_weight,
    bias_qv,
    output_weight,
    bias_out,
    gain_one,
    shift_one,
    gain_two,
    shift_two,
    up_weight,
    bias_up,
    down_weight,
    bias_down,
    out_grad,
):
    scale_query = HDIM ** (-0.5)
    inputs = block_in.astype(jnp.float32)
    normed_one, centred_one, inverse_one = norm_forward(inputs, gain_one, shift_one)
    normed_one = normed_one.astype(jnp.bfloat16)
    first_rows = gather_rows(normed_one)
    projected = summed_column_block(
        jnp.einsum(
            "mhu,fxu->mhfx", first_rows, query_key_value_weight, preferred_element_type=jnp.float32
        )
    )
    bias_full = jnp.stack([bias_qv[0], jnp.zeros_like(bias_qv[0]), bias_qv[1]])
    projected = (projected + bias_full).astype(jnp.bfloat16)
    heads_local = spread_queries(projected)
    keyval = collect_keys(projected)
    query = heads_local[:, :, 0] * scale_query
    length = keyval.shape[1]
    rows_here = query.shape[1]
    positions = lax.axis_index(ROW) * rows_here + jnp.arange(rows_here)
    causal = positions[:, None] >= jnp.arange(length)[None, :]
    count_heads = query.shape[2] // HDIM
    keys_all = keyval[:, :, 0]
    values_all = keyval[:, :, 1]

    def head_forward(head):
        query_head = head_slice(query, head, 2)
        key_head = head_slice(keys_all, head, 2)
        value_head = head_slice(values_all, head, 2)
        scores = jnp.einsum(
            "pqd,pkd->pqk", query_head, key_head, preferred_element_type=jnp.float32
        )
        scores = jnp.where(causal, scores, MASKED)
        highest = jnp.max(scores, axis=-1, keepdims=True)
        exponent = jnp.exp(scores - highest)
        summed = jnp.sum(exponent, axis=-1, keepdims=True)
        weights = (exponent / summed).astype(jnp.bfloat16)
        mixed_head = jnp.einsum(
            "pqk,pkd->pqd", weights, value_head, preferred_element_type=jnp.float32
        )
        return (mixed_head, highest + jnp.log(summed))

    mixed_heads, log_totals = lax.map(head_forward, jnp.arange(count_heads))
    mixed = jnp.transpose(mixed_heads, (1, 2, 0, 3)).reshape(query.shape).astype(jnp.bfloat16)
    mixed_columns = from_heads(mixed[:, :, None])[:, :, 0]
    mixed_full = gather_columns(mixed_columns)
    attended = (
        summed_row_block(
            jnp.einsum("nfm,mc->nfc", mixed_full, output_weight, preferred_element_type=jnp.float32)
        )
        + bias_out
    )
    residual = inputs + attended
    normed_two, centred_two, inverse_two = norm_forward(residual, gain_two, shift_two)
    normed_two = normed_two.astype(jnp.bfloat16)
    second_rows = gather_rows(normed_two)
    hidden = (
        summed_column_block(
            jnp.einsum("bae,we->baw", second_rows, up_weight, preferred_element_type=jnp.float32)
        )
        + bias_up
    )
    active = jax.nn.gelu(hidden, approximate=False).astype(jnp.bfloat16)
    active_full = gather_columns(active)
    lowered = (
        summed_row_block(
            jnp.einsum("epa,ao->epo", active_full, down_weight, preferred_element_type=jnp.float32)
        )
        + bias_down
    )
    block_out = (residual + lowered).astype(jnp.bfloat16)
    gradient_rows = gather_rows(out_grad)
    grad_bias_down = jnp.sum(gradient_rows, axis=(0, 1), dtype=jnp.float32)
    down_weight_gradient = jnp.einsum(
        "rjk,rjb->kb", active_full, gradient_rows, preferred_element_type=jnp.float32
    )
    d_active = summed_column_block(
        jnp.einsum("bae,we->baw", gradient_rows, down_weight, preferred_element_type=jnp.float32)
    )
    d_hidden = (d_active * gelu_slope(hidden)).astype(jnp.bfloat16)
    hidden_full = gather_columns(d_hidden)
    grad_bias_up = jnp.sum(hidden_full, axis=(0, 1), dtype=jnp.float32)
    up_weight_gradient = jnp.einsum(
        "rjk,rjb->kb", hidden_full, second_rows, preferred_element_type=jnp.float32
    )
    d_normed_two = summed_row_block(
        jnp.einsum("epa,ao->epo", hidden_full, up_weight, preferred_element_type=jnp.float32)
    )
    resid_part, grad_gain_two, grad_shift_two = norm_backward(
        d_normed_two, centred_two, inverse_two, gain_two
    )
    d_residual = out_grad.astype(jnp.float32) + resid_part
    d_attended = d_residual.astype(jnp.bfloat16)
    attended_token_rows = gather_rows(d_attended)
    grad_bias_out = jnp.sum(attended_token_rows, axis=(0, 1), dtype=jnp.float32)
    grad_out = jnp.einsum(
        "xar,xav->rv", mixed_full, attended_token_rows, preferred_element_type=jnp.float32
    )
    d_mixed = summed_column_block(
        jnp.einsum(
            "nue,ze->nuz", attended_token_rows, output_weight, preferred_element_type=jnp.float32
        )
    )
    d_mixed = to_heads(d_mixed.astype(jnp.bfloat16)[:, :, None])[:, :, 0]

    def head_backward(head):
        query_head = head_slice(query, head, 2)
        key_head = head_slice(keys_all, head, 2)
        value_head = head_slice(values_all, head, 2)
        upstream = head_slice(d_mixed, head, 2)
        scores = jnp.einsum(
            "pqd,pkd->pqk", query_head, key_head, preferred_element_type=jnp.float32
        )
        scores = jnp.where(causal, scores, MASKED)
        probs = jnp.exp(scores - log_totals[head])
        d_probs = jnp.einsum(
            "pqd,pkd->pqk", upstream, value_head, preferred_element_type=jnp.float32
        )
        centre = jnp.sum(probs * d_probs, axis=-1, keepdims=True)
        d_scores = (probs * (d_probs - centre)).astype(jnp.bfloat16)
        d_query = (
            jnp.einsum("pqk,pkd->pqd", d_scores, key_head, preferred_element_type=jnp.float32)
            * scale_query
        )
        d_key = jnp.einsum("pqk,pqd->pkd", d_scores, query_head, preferred_element_type=jnp.float32)
        d_value = jnp.einsum(
            "pqk,pqd->pkd", probs.astype(jnp.bfloat16), upstream, preferred_element_type=jnp.float32
        )
        return (d_query, d_key, d_value)

    query_grads, key_grads, value_grads = lax.map(head_backward, jnp.arange(count_heads))
    query_grads = jnp.transpose(query_grads, (1, 2, 0, 3)).reshape(query.shape).astype(jnp.bfloat16)
    query_columns = from_heads(query_grads[:, :, None])
    pair_grads = jnp.transpose(jnp.stack([key_grads, value_grads]), (2, 3, 0, 1, 4))
    pair_grads = pair_grads.reshape(pair_grads.shape[0], pair_grads.shape[1], 2, query.shape[2])
    pair_columns = lax.psum_scatter(pair_grads, ROW, scatter_dimension=3, tiled=True).astype(
        jnp.bfloat16
    )
    d_projected = jnp.concatenate([query_columns, pair_columns], axis=2)
    projected_full = gather_columns(d_projected)
    bias_sums = jnp.sum(projected_full, axis=(0, 1), dtype=jnp.float32)
    grad_bias_qv = jnp.stack([bias_sums[0], bias_sums[2]])
    grad_qkv = jnp.einsum(
        "urbf,ure->bfe", projected_full, first_rows, preferred_element_type=jnp.float32
    )
    d_normed_one = summed_row_block(
        jnp.einsum(
            "znce,cer->znr",
            projected_full,
            query_key_value_weight,
            preferred_element_type=jnp.float32,
        )
    )
    input_part, grad_gain_one, grad_shift_one = norm_backward(
        d_normed_one, centred_one, inverse_one, gain_one
    )
    in_grad = d_residual + input_part
    grad_gain_one, grad_shift_one, grad_gain_two, grad_shift_two = in_one(
        (grad_gain_one, grad_shift_one, grad_gain_two, grad_shift_two), DP_ROW
    )
    (
        grad_qkv,
        grad_bias_qv,
        grad_out,
        grad_bias_out,
        up_weight_gradient,
        grad_bias_up,
        down_weight_gradient,
        grad_bias_down,
    ) = lax.psum(
        (
            grad_qkv,
            grad_bias_qv,
            grad_out,
            grad_bias_out,
            up_weight_gradient,
            grad_bias_up,
            down_weight_gradient,
            grad_bias_down,
        ),
        "dp",
    )
    return (
        block_out,
        in_grad,
        grad_qkv,
        grad_bias_qv,
        grad_out,
        grad_bias_out,
        grad_gain_one,
        grad_shift_one,
        grad_gain_two,
        grad_shift_two,
        up_weight_gradient,
        grad_bias_up,
        down_weight_gradient,
        grad_bias_down,
    )


def solution(mesh):
    finer = Mesh(
        mesh.devices.reshape(mesh.shape["dp"], 4, 2, mesh.shape["col"]),
        ("dp", "row_0", "row_1", "col"),
    )
    return jax.shard_map(
        per_device,
        mesh=finer,
        in_specs=(
            P("dp", ROW, "col"),
            P(None, ROW, "col"),
            P(None, ROW),
            P(ROW, "col"),
            P("col"),
            P("col"),
            P("col"),
            P("col"),
            P("col"),
            P(ROW, "col"),
            P(ROW),
            P(ROW, "col"),
            P("col"),
            P("dp", ROW, "col"),
        ),
        out_specs=(
            P("dp", ROW, "col"),
            P("dp", ROW, "col"),
            P(None, ROW, "col"),
            P(None, ROW),
            P(ROW, "col"),
            P("col"),
            P("col"),
            P("col"),
            P("col"),
            P("col"),
            P(ROW, "col"),
            P(ROW),
            P(ROW, "col"),
            P("col"),
        ),
        check_vma=False,
    )
```

profile of v0, /device:TPU:6, one launch (start us, length us, event | category | flops | bytes accessed | tf_op | source)
XLA Modules:
  0.0 1212.2 jit_solution(742849915010569095)
XLA Ops:
  14.8 8.2 all-to-all-start
  23.2 30.3 %all-to-all-done = bf16[8,2,128,544]{2,3,1,0:T(8,128)(2,1)S(1)} async-done(((bf16[8,2,128,544]{2,3,1,0:T(8,128)(2,1)}), bf16[8,2,128,544]{2,3,1,0:T(8,128)(2,1)S(1)}, u32[]{:S(2)}, u32[]{:S(2)}) %all-to-all-start) | async-done | bytes 2228256 | tf_op jit(solution)/shard_map/all_to_all | solution.py:22
  61.4 6.4 all_to_all.123
  77.3 6.7 all-to-all-start.2
  84.2 8.6 all-to-all-done.2
  95.5 50.2 %all-gather.18.cloned.1.call-done = bf16[1,1024,2,1088]{1,2,0,3:T(2,128)(2,1)} async-done(((bf16[1,1024,2,136]{1,2,0,3:T(2,128)(2,1)}), bf16[1,1024,2,1088]{1,2,0,3:T(2,128)(2,1)}) %all-gather.18.cloned.1.call-update) | async-done | bytes 4456464 | tf_op jit(solution)/shard_map/all_gather | solution.py:101
  145.8 9.3 fusion.148
  164.6 74.7 %while.28 = (s32[]{:T(128)}, bf16[17,1,128,64]{2,3,1,0:T(8,128)(2,1)}, f32[17,1,128,1]{2,3,1,0:T(1,128)}, s32[17]{0:T(128)S(1)}, bf16[1,128,1088]{2,1,0:T(8,128)...) while((s32[]{:T(128)}, ...), condition=%wide.region_8.9_spmd.clone, body=%wide.region_5.8_spmd.clone.sunk | while | flops 34602884 | bytes 2168515 | solution.py:189
  243.3 8.1 reduce.22
  253.2 13.4 %all_to_all.124 = bf16[8,2,8704]{2,1,0:T(2,128)(2,1)} all-to-all(bf16[8,2,8704]{2,1,0:T(2,128)(2,1)} %reshape.596), channel_id=1, replica_groups=mesh['dp'=8,'row_0'=4,'row_1'=2,'col'=2] {'row_0','row_1'}, dimensions={0} | all-to-all | bytes 557056 | tf_op jit(solution)/shard_map/all_to_all | solution.py:93
  280.2 6.3 all-to-all-start.8
  286.5 60.7 %reduce-scatter.10.cloned.1.call-done = f32[2,256,544]{1,2,0:T(8,128)} async-done(((f32[2,1024,544]{1,2,0:T(8,128)}), f32[2,256,544]{1,2,0:T(8,128)}) %reduce-scatter.10.cloned.1.call-update) | async-done | bytes 1114128 | tf_op jit(solution)/shard_map/reduce_scatter | solution.py:51
  347.3 5.8 fusion.85
  353.1 6.2 all-to-all-start.9
  359.4 17.1 %reduce-scatter.12.cloned.1.call-done = f32[2,128,544]{1,2,0:T(8,128)} async-done(((f32[2,256,544]{1,2,0:T(8,128)}), f32[2,128,544]{1,2,0:T(8,128)}) %reduce-scatter.12.cloned.1.call-update) | async-done | bytes 557072 | tf_op jit(solution)/shard_map/reduce_scatter | solution.py:51
  395.9 26.8 %all-to-all-done.5 = bf16[8,2,128,544]{2,3,1,0:T(8,128)(2,1)} async-done(((bf16[8,2,128,544]{2,3,1,0:T(8,128)(2,1)}), bf16[8,2,128,544]{2,3,1,0:T(8,128)(2,1)}, u32[]{:S(2)}, u32[]{:S(2)}) %all-to-all-start.5) | async-done | bytes 2228256 | tf_op jit(solution)/shard_map/all_to_all | solution.py:22
  426.2 8.4 all_to_all.126
  438.9 8.1 fusion.52
  458.3 48.0 %reduce-scatter.18.cloned.1.call-done = f32[2,256,544]{1,2,0:T(8,128)} async-done(((f32[2,1024,544]{1,2,0:T(8,128)}), f32[2,256,544]{1,2,0:T(8,128)}) %reduce-scatter.18.cloned.1.call-update) | async-done | bytes 1114128 | tf_op jit(solution)/shard_map/reduce_scatter | solution.py:51
  506.3 29.1 %reduce-scatter.20.cloned.1.call-done = f32[2,128,544]{1,2,0:T(8,128)} async-done(((f32[2,256,544]{1,2,0:T(8,128)}), f32[2,128,544]{1,2,0:T(8,128)}) %reduce-scatter.20.cloned.1.call-update) | async-done | bytes 557072 | tf_op jit(solution)/shard_map/reduce_scatter | solution.py:51
  542.1 32.5 %all_to_all.132 = bf16[8,2,128,544]{2,3,1,0:T(8,128)(2,1)S(1)} all-to-all(bf16[8,2,128,544]{2,3,1,0:T(8,128)(2,1)S(1)} %broadcast_in_dim.59), channel_id=1, replica_groups=mesh['dp'=8,'row_0'=4,'row_1'=2,'col'=2] {'row_0','row_1'}, dimensions={0} | all-to-all | bytes 4456448 | tf_op jit(solution)/shard_map/all_to_all | solution.py:22
  597.6 7.0 all-to-all-done.13
  611.1 184.1 %while.29 = (s32[]{:T(128)}, bf16[17,1,128,64]{2,3,1,0:T(8,128)(2,1)}, f32[17,1,1024,64]{2,3,1,0:T(8,128)}, f32[17,1,1024,64]{2,3,1,0:T(8,128)}, s32[17]{0:T(128...) while((s32[]{:T(128)}, ...), condition=%wide.region_28.29_spmd.clone, body=%wide.region_26.28_spmd.clone.sunk | while | flops 85073792 | bytes 5379349 | solution.py:277
  795.2 8.8 pad_maximum_fusion
  809.3 6.4 reduce.24
  815.8 13.7 %all_to_all.129 = bf16[8,2,8704]{2,1,0:T(2,128)(2,1)S(1)} all-to-all(bf16[8,2,8704]{2,1,0:T(2,128)(2,1)S(1)} %reshape.600), channel_id=1, replica_groups=mesh['dp'=8,'row_0'=4,'row_1'=2,'col'=2] {'row_0','row_1'}, dimensions={0} | all-to-all | bytes 557056 | tf_op jit(solution)/shard_map/all_to_all | solution.py:93
  829.9 95.6 %reduce-scatter.22.cloned.1.call-done = f32[1,1024,2,136]{1,3,2,0:T(8,128)} async-done(((f32[1,1024,2,1088]{1,3,2,0:T(8,128)}), f32[1,1024,2,136]{1,3,2,0:T(8,128)}) %reduce-scatter.22.cloned.1.call-update) | async-done | bytes 1114128 | tf_op jit(solution)/shard_map/reduce_scatter | solution.py:282
  948.6 33.8 %reduce-scatter.24.cloned.1.call-done = f32[2,256,544]{1,2,0:T(8,128)} async-done(((f32[2,1024,544]{1,2,0:T(8,128)}), f32[2,256,544]{1,2,0:T(8,128)}) %reduce-scatter.24.cloned.1.call-update) | async-done | bytes 1114128 | tf_op jit(solution)/shard_map/reduce_scatter | solution.py:51
  982.6 51.2 %reduce-scatter.14.cloned.1.call-done = f32[2,256,544]{1,2,0:T(8,128)} async-done(((f32[2,1024,544]{1,2,0:T(8,128)}), f32[2,256,544]{1,2,0:T(8,128)}) %reduce-scatter.14.cloned.1.call-update) | async-done | bytes 1114128 | tf_op jit(solution)/shard_map/reduce_scatter | solution.py:51
  1052.2 35.4 %all-reduce = (f32[2,136]{1,0:T(2,128)}, f32[544]{0:T(1024)}, f32[544]{0:T(1024)}, f32[544]{0:T(1024)}) all-reduce(f32[2,136]{1,0:T(2,128)S(1)} %pad_maximum_fusion.2, f32[544]{0:T(1024)S(1)} %convert_reduce_fusion.2, f32[544]{0:T(1024)S(1)} %convert_reduce_fusion.1, ...), channel_id=1, replica_groups=mesh['dp'=8,'row_0'=4,'row_1'=2,'col'=2] {'dp'}, use_global_device_ids=true, to_apply=%region_38.39 | all-reduce | flops 1904 | bytes 15232 | tf_op jit(solution)/shard_map/psum | solution.py:316
  1090.3 7.8 all-to-all-start.16
  1109.7 90.2 %all-reduce.4.cloned.1.call-done = (f32[3,136,544]{2,1,0:T(8,128)}, f32[136,544]{1,0:T(8,128)}, f32[544,544]{1,0:T(8,128)}, f32[544,544]{1,0:T(8,128)}) async-done(((f32[3,136,544]{2,1,0:T(8,128)}, f32[136,544]{1,0:T(8,128)}, f32[544,544]{1,0:T(8,128)}, f32[544,544]{1,0:T(8,128)}), (f32[3,136,544]{2,1,0:T(8,128)}, f32[136,544]{1,0:T(8,128)}, f32[544,544]{1,0:T(8,128)}, ...) | async-done | bytes 3551248 | tf_op jit(solution)/shard_map/psum | solution.py:316
  (444 shorter events, 401.5 us)
Async XLA Ops:
  7.2 415.5 %copy-start = (bf16[544,544]{1,0:T(8,128)(2,1)S(1)}, bf16[544,544]{1,0:T(8,128)(2,1)}, u32[]{:S(2)}) copy-start(bf16[544,544]{1,0:T(8,128)(2,1)} %param.27) | copy-start | bytes 1775620
  14.8 8.3 copy-start.34
  14.8 38.7 %all-to-all-start = ((bf16[8,2,128,544]{2,3,1,0:T(8,128)(2,1)}), bf16[8,2,128,544]{2,3,1,0:T(8,128)(2,1)S(1)}, u32[]{:S(2)}, u32[]{:S(2)}) async-start(bf16[8,2,128,544]{2,3,1,0:T(8,128)(2,1)} %broadcast_in_dim.52), calls=%async_computation | async-start | bytes 4456448 | tf_op jit(solution)/shard_map/all_to_all | solution.py:22
  23.0 122.8 %all-gather.18.cloned.1.call-start = ((), (), s32[]{:S(2)}) async-start(), calls=%async_computation.26 | async-start | bytes 5013504 | tf_op jit(solution)/shard_map/all_gather | solution.py:101
  77.3 15.5 %all-to-all-start.2 = ((bf16[8,2,8704]{2,1,0:T(2,128)(2,1)}), bf16[8,2,8704]{2,1,0:T(2,128)(2,1)S(1)}, u32[]{:S(2)}, u32[]{:S(2)}) async-start(bf16[8,2,8704]{2,1,0:T(2,128)(2,1)} %reshape.594), calls=%async_computation.2 | async-start | bytes 557056 | tf_op jit(solution)/shard_map/all_to_all | solution.py:89
  84.0 263.2 %reduce-scatter.10.cloned.1.call-start = ((), (), s32[]{:S(2)}) async-start(), calls=%async_computation.27 | async-start | bytes 5570560 | tf_op jit(solution)/shard_map/reduce_scatter | solution.py:51
  239.3 30.3 %copy-start.20 = (bf16[1,128,1088]{2,1,0:T(8,128)(2,1)}, bf16[1,128,1088]{2,1,0:T(8,128)(2,1)S(1)}, u32[]{:S(2)}) copy-start(bf16[1,128,1088]{2,1,0:T(8,128)(2,1)S(1)} %get-tuple-element.648) | copy-start | bytes 835588
  280.2 67.1 %all-to-all-start.8 = ((bf16[8,2,128,544]{2,3,1,0:T(8,128)(2,1)}), bf16[8,2,128,544]{2,3,1,0:T(8,128)(2,1)}, u32[]{:S(2)}, u32[]{:S(2)}) async-start(bf16[8,2,128,544]{2,3,1,0:T(8,128)(2,1)} %broadcast_in_dim.57), calls=%async_computation.12 | async-start | bytes 4456448 | tf_op jit(solution)/shard_map/all_to_all | solution.py:22
  286.5 89.9 %reduce-scatter.12.cloned.1.call-start = ((), (), s32[]{:S(2)}) async-start(), calls=%async_computation.28 | async-start | bytes 1671168 | tf_op jit(solution)/shard_map/reduce_scatter | solution.py:51
  353.1 23.3 %copy-start.9 = (bf16[2,128,544]{1,2,0:T(8,128)(2,1)S(1)}, bf16[2,128,544]{1,2,0:T(8,128)(2,1)}, u32[]{:S(2)}) copy-start(bf16[2,128,544]{1,2,0:T(8,128)(2,1)} %param.18) | copy-start | bytes 835588
  353.1 23.3 %copy-start.30 = (f32[544]{0:T(1024)S(1)}, f32[544]{0:T(1024)}, u32[]{:S(2)}) copy-start(f32[544]{0:T(1024)} %param.22) | copy-start | bytes 6532
  353.1 28.9 %copy-start.28 = (f32[544]{0:T(1024)S(1)}, f32[544]{0:T(1024)}, u32[]{:S(2)}) copy-start(f32[544]{0:T(1024)} %param.25) | copy-start | bytes 6532
  353.1 28.9 %copy-start.31 = (f32[544]{0:T(1024)S(1)}, f32[544]{0:T(1024)}, u32[]{:S(2)}) copy-start(f32[544]{0:T(1024)} %param.26) | copy-start | bytes 6532
  353.1 30.9 %all-to-all-start.9 = ((f32[2,1,1024,544]{2,3,1,0:T(8,128)}), f32[2,1,1024,544]{2,3,1,0:T(8,128)}, u32[]{:S(2)}, u32[]{:S(2)}) async-start(f32[2,1,1024,544]{2,3,1,0:T(8,128)} %fusion.85), calls=%async_computation.13 | async-start | bytes 8912896 | tf_op jit(solution)/shard_map/all_to_all | solution.py:44
  386.7 35.9 %all-to-all-start.5 = ((bf16[8,2,128,544]{2,3,1,0:T(8,128)(2,1)}), bf16[8,2,128,544]{2,3,1,0:T(8,128)(2,1)}, u32[]{:S(2)}, u32[]{:S(2)}) async-start(bf16[8,2,128,544]{2,3,1,0:T(8,128)(2,1)} %broadcast_in_dim.55), calls=%async_computation.7 | async-start | bytes 4456448 | tf_op jit(solution)/shard_map/all_to_all | solution.py:22
  391.6 114.7 %reduce-scatter.18.cloned.1.call-start = ((), (), s32[]{:S(2)}) async-start(), calls=%async_computation.31 | async-start | bytes 5570560 | tf_op jit(solution)/shard_map/reduce_scatter | solution.py:51
  458.2 77.2 %copy-start.2 = (f32[2,128,544]{1,2,0:T(8,128)S(1)}, f32[2,128,544]{1,2,0:T(8,128)}, u32[]{:S(2)}) copy-start(f32[2,128,544]{1,2,0:T(8,128)} %get-tuple-element.356) | copy-start | bytes 1671172
  458.2 77.2 %reduce-scatter.20.cloned.1.call-start = ((), (), s32[]{:S(2)}) async-start(), calls=%async_computation.32 | async-start | bytes 1671168 | tf_op jit(solution)/shard_map/reduce_scatter | solution.py:51
  592.1 12.4 %all-to-all-start.13 = ((bf16[8,2,8704]{2,1,0:T(2,128)(2,1)}), bf16[8,2,8704]{2,1,0:T(2,128)(2,1)S(1)}, u32[]{:S(2)}, u32[]{:S(2)}) async-start(bf16[8,2,8704]{2,1,0:T(2,128)(2,1)} %reshape.598), calls=%async_computation.19 | async-start | bytes 557056 | tf_op jit(solution)/shard_map/all_to_all | solution.py:89
  597.6 327.9 %reduce-scatter.22.cloned.1.call-start = ((), (), s32[]{:S(2)}) async-start(), calls=%async_computation.33 | async-start | bytes 10027008 | tf_op jit(solution)/shard_map/reduce_scatter | solution.py:282
  804.0 178.5 %reduce-scatter.24.cloned.1.call-start = ((), (), s32[]{:S(2)}) async-start(), calls=%async_computation.34 | async-start | bytes 5570560 | tf_op jit(solution)/shard_map/reduce_scatter | solution.py:51
  935.7 98.0 %reduce-scatter.14.cloned.1.call-start = ((), (), s32[]{:S(2)}) async-start(), calls=%async_computation.29 | async-start | bytes 5570560 | tf_op jit(solution)/shard_map/reduce_scatter | solution.py:51
  948.6 139.0 %reduce-scatter.26.cloned.1.call-start = ((), (), s32[]{:S(2)}) async-start(), calls=%async_computation.35 | async-start | bytes 1671168 | tf_op jit(solution)/shard_map/reduce_scatter | solution.py:51
  982.5 119.2 %reduce-scatter.16.cloned.1.call-start = ((), (), s32[]{:S(2)}) async-start(), calls=%async_computation.30 | async-start | bytes 1671168 | tf_op jit(solution)/shard_map/reduce_scatter | solution.py:51
  1033.8 166.2 %all-reduce.4.cloned.1.call-start = ((), (), s32[]{:S(2)}) async-start(), calls=%async_computation.36 | async-start | bytes 8355840 | tf_op jit(solution)/shard_map/psum | solution.py:316
  1051.5 36.1 %copy-start.29 = (f32[544]{0:T(1024)S(1)}, f32[544]{0:T(1024)}, u32[]{:S(2)}) copy-start(f32[544]{0:T(1024)} %param.23) | copy-start | bytes 6532
  1051.9 49.9 %copy-start.3 = (f32[2,128,544]{1,2,0:T(8,128)S(1)}, f32[2,128,544]{1,2,0:T(8,128)}, u32[]{:S(2)}) copy-start(f32[2,128,544]{1,2,0:T(8,128)} %get-tuple-element.356) | copy-start | bytes 1671172
  1051.9 49.9 %copy-start.10 = (f32[2,128,544]{1,2,0:T(8,128)S(1)}, f32[2,128,544]{1,2,0:T(8,128)}, u32[]{:S(2)}) copy-start(f32[2,128,544]{1,2,0:T(8,128)} %reduce-scatter.20.cloned.1.call-done) | copy-start | bytes 1671172
  1051.9 49.9 %copy-start.33 = (f32[544]{0:T(1024)S(1)}, f32[544]{0:T(1024)}, u32[]{:S(2)}) copy-start(f32[544]{0:T(1024)} %param.30) | copy-start | bytes 6532
  1052.2 49.6 %copy-start.12 = (bf16[2,128,544]{1,2,0:T(8,128)(2,1)S(1)}, bf16[2,128,544]{1,2,0:T(8,128)(2,1)}, u32[]{:S(2)}) copy-start(bf16[2,128,544]{1,2,0:T(8,128)(2,1)} %param.31) | copy-start | bytes 835588
  1087.6 14.2 %copy-start.19 = (f32[2,128,544]{1,2,0:T(8,128)S(1)}, f32[2,128,544]{1,2,0:T(8,128)}, u32[]{:S(2)}) copy-start(f32[2,128,544]{1,2,0:T(8,128)} %reduce-scatter.26.cloned.1.call-done) | copy-start | bytes 1671172
  1090.3 18.4 %all-to-all-start.16 = ((f32[64,1,2176]{2,1,0:T(1,128)}), f32[64,1,2176]{2,1,0:T(1,128)S(1)}, u32[]{:S(2)}, u32[]{:S(2)}) async-start(f32[64,1,2176]{2,1,0:T(1,128)} %broadcast_in_dim.64), calls=%async_computation.25 | async-start | bytes 1114112 | tf_op jit(solution)/shard_map/all_to_all | solution.py:22
  (22 other events, 69.0 us)
Sparse Core Ops, SparseCore 0:
  70.0 75.6 all-gather.17
  277.7 69.4 reduce-scatter.9
  349.6 26.7 reduce-scatter.11
  458.3 47.8 reduce-scatter.17
  508.6 26.7 reduce-scatter.19
  804.2 121.2 reduce-scatter.21
  935.8 46.6 reduce-scatter.23
  985.0 48.6 reduce-scatter.13
  1036.2 26.8 reduce-scatter.25
  1065.4 24.4 reduce-scatter.15
  1094.1 105.8 all-reduce.3
where the time goes:
time: 1230 us; the launch traced here: 1210 us
  waiting for transfers between devices  553 us (45%)
  matrix products  197 us (16%)
  blocking collectives  150 us (12%)
  local copies, waits for them, and re-layouts  110 us (9%)
  other arithmetic  85.1 us (7%)
  loops' own time  55.7 us (5%)
  starting transfers between devices  46.6 us (4%)
  between operations  14.9 us (1%)
    reduce_scatter x8, waiting for transfers between devices, scatter_axes(): nearer = lax.psum_scatter(x, axes[0], scatter_dimension=dim, tiled=True)  240 us
    reduce_scatter x1, waiting for transfers between devices, per_device(): lax.psum_scatter(pair_grads, ROW, scatter_dimension=3, tiled=True)  95.6 us
    psum x1, waiting for transfers between devices, per_device(): lax.psum((grad_qkv, grad_bias_qv, grad_out, grad_bias_out, up_weight_grad...  90.2 us
    all_to_all x4, waiting for transfers between devices, sent_to_all(): lax.all_to_all(jnp.broadcast_to(x[None], (size, *x.shape)), axis, 0, 0, t...  61.6 us
    all_to_all x5, blocking collectives, sent_to_all(): lax.all_to_all(jnp.broadcast_to(x[None], (size, *x.shape)), axis, 0, 0, t...  53 us
    all_gather x1, waiting for transfers between devices, collect_keys(): return lax.all_gather(projected[:, :, 1:3], ROW, axis=3, tiled=True)  50.2 us
    another operation x1, loops' own time, per_device(): lax.map(head_backward, jnp.arange(count_heads))  44.4 us
    psum x1, blocking collectives, per_device(): lax.psum((grad_qkv, grad_bias_qv, grad_out, grad_bias_out, up_weight_grad...  35.4 us
  transfers between devices with their start and end apart: 18, of which 14 were waited for; matrix products, arithmetic and copies ran while one was open for 6% of the time, Pallas kernels for 0%

commit v1 on v0

v1 whole, which is shorter than its diff:
```python
import functools

import jax
import jax.numpy as jnp
from jax import lax
from jax.experimental import pallas as pl
from jax.experimental.pallas import tpu as pltpu
from jax.sharding import Mesh
from jax.sharding import PartitionSpec as P


HDIM = 64
D = 1088
HALF = D // 2
TOK = 128
LEN = 1024
SLOT = 192
EPSILON = 1e-05
MASKED = -1e30
DP = ("zl", "y")
ROW = ("x", "zh")
ALL = ("zl", "y", "x", "zh", "c")
MESH = pl.DeviceIdType.MESH
BF = jnp.bfloat16
F32 = jnp.float32


def greet(targets):
    barrier = pltpu.get_barrier_semaphore()
    for target in targets:
        pl.semaphore_signal(barrier, inc=1, device_id=target, device_id_type=MESH)
    pl.semaphore_wait(barrier, len(targets))


def remote(src, dst, send, recv, target):
    return pltpu.make_async_remote_copy(
        src_ref=src, dst_ref=dst, send_sem=send, recv_sem=recv, device_id=target, device_id_type=MESH
    )


def gather_kernel(a_ref, o_ref, own_sem, x_send, x_recv, c_send, c_recv):
    x, c = lax.axis_index("x"), lax.axis_index("c")
    sibling = {"c": 1 - c}
    greet([{"x": lax.rem(x + k, 4)} for k in (1, 2, 3)] + [sibling])
    own = 2 * x + c
    kept = pltpu.make_async_copy(a_ref, o_ref.at[own], own_sem)
    kept.start()
    far = {}
    for k in (1, 3, 2):
        far[k] = remote(a_ref, o_ref.at[own], x_send.at[k], x_recv.at[k], {"x": lax.rem(x + k, 4)})
        far[k].start()
    near = [remote(a_ref, o_ref.at[own], c_send.at[0], c_recv.at[0], sibling)]
    near[0].start()
    for k in (1, 3, 2):
        far[k].wait_recv()
        slot = 2 * lax.rem(x + 4 - k, 4) + c
        copy = remote(o_ref.at[slot], o_ref.at[slot], c_send.at[k], c_recv.at[k], sibling)
        copy.start()
        near.append(copy)
    kept.wait()
    for copy in near:
        copy.wait()
    for k in (1, 3, 2):
        far[k].wait_send()


def line_gather(a, cid):
    return pl.pallas_call(
        gather_kernel,
        out_shape=jax.ShapeDtypeStruct((8, *a.shape), a.dtype),
        in_specs=[pl.BlockSpec(memory_space=pltpu.VMEM)],
        out_specs=pl.BlockSpec(memory_space=pltpu.VMEM),
        scratch_shapes=[pltpu.SemaphoreType.DMA] + [pltpu.SemaphoreType.DMA((4,))] * 4,
        compiler_params=pltpu.CompilerParams(
            collective_id=cid, has_side_effects=True, vmem_limit_bytes=32 << 20
        ),
        name="line_gather",
    )(a)


def scatter_kernel(p_ref, o_ref, near, out, arrived, c_send, c_recv, x_send, x_recv):
    x, c = lax.axis_index("x"), lax.axis_index("c")
    sibling = {"c": 1 - c}
    greet([{"x": lax.rem(x + k, 4)} for k in (1, 2, 3)] + [sibling])
    order = (2, 1, 3, 0)
    swaps, sends = {}, {}
    for k in order:
        to = lax.rem(x + k, 4)
        swaps[k] = remote(p_ref.at[2 * to + 1 - c], near.at[k], c_send.at[k], c_recv.at[k], sibling)
        swaps[k].start()
    for k in order:
        to = lax.rem(x + k, 4)
        swaps[k].wait_recv()
        both = p_ref[2 * to + c].astype(F32) + near[k].astype(F32)
        if k == 0:
            o_ref[...] = both
        else:
            out[k] = both.astype(BF)
            sends[k] = remote(out.at[k], arrived.at[k], x_send.at[k], x_recv.at[k], {"x": to})
            sends[k].start()
    for k in (1, 3, 2):
        sends[k].wait_recv()
        o_ref[...] += arrived[k].astype(F32)
    for k in (1, 3, 2):
        sends[k].wait_send()
    for k in order:
        swaps[k].wait_send()


def line_scatter(p, cid):
    return pl.pallas_call(
        scatter_kernel,
        out_shape=jax.ShapeDtypeStruct(p.shape[1:], F32),
        in_specs=[pl.BlockSpec(memory_space=pltpu.VMEM)],
        out_specs=pl.BlockSpec(memory_space=pltpu.VMEM),
        scratch_shapes=[pltpu.VMEM((4, *p.shape[1:]), BF)] * 3 + [pltpu.SemaphoreType.DMA((4,))] * 4,
        compiler_params=pltpu.CompilerParams(
            collective_id=cid, has_side_effects=True, vmem_limit_bytes=32 << 20
        ),
        name="line_scatter",
    )(p)


def others(x, c):
    return [(k, j, lax.rem(x + k, 4), lax.rem(c + j, 2)) for k, j in ((2, 0), (2, 1), (1, 0), (1, 1), (3, 0), (3, 1), (0, 1))]


def to_tokens_kernel(m_ref, o_ref, own_sem, send, recv):
    x, c = lax.axis_index("x"), lax.axis_index("c")
    peers = others(x, c)
    greet([{"x": xx, "c": cc} for _, _, xx, cc in peers])
    own = 2 * x + c
    columns = pl.ds(pl.multiple_of(own * TOK, TOK), TOK)
    kept = pltpu.make_async_copy(m_ref.at[:, columns], o_ref.at[own], own_sem)
    kept.start()
    copies = []
    for k, j, xx, cc in peers:
        columns = pl.ds(pl.multiple_of((2 * xx + cc) * TOK, TOK), TOK)
        n = 2 * k + j
        copy = remote(m_ref.at[:, columns], o_ref.at[own], send.at[n], recv.at[n], {"x": xx, "c": cc})
        copy.start()
        copies.append(copy)
    kept.wait()
    for copy in copies:
        copy.wait()


def to_tokens(m, cid):
    return pl.pallas_call(
        to_tokens_kernel,
        out_shape=jax.ShapeDtypeStruct((8, SLOT, TOK), BF),
        in_specs=[pl.BlockSpec(memory_space=pltpu.VMEM)],
        out_specs=pl.BlockSpec(memory_space=pltpu.VMEM),
        scratch_shapes=[pltpu.SemaphoreType.DMA] + [pltpu.SemaphoreType.DMA((8,))] * 2,
        compiler_params=pltpu.CompilerParams(
            collective_id=cid, has_side_effects=True, vmem_limit_bytes=32 << 20
        ),
        name="to_tokens",
    )(m)


def to_heads_kernel(m_ref, o_ref, own_sem, send, recv):
    x, c = lax.axis_index("x"), lax.axis_index("c")
    peers = others(x, c)
    greet([{"x": xx, "c": cc} for _, _, xx, cc in peers])
    own = 2 * x + c
    columns = pl.ds(pl.multiple_of(own * TOK, TOK), TOK)

    def rows(rank):
        return pl.ds(pl.multiple_of(rank * 2 * HDIM, 2 * HDIM), SLOT)

    kept = pltpu.make_async_copy(m_ref.at[rows(own)], o_ref.at[:, columns], own_sem)
    kept.start()
    copies = []
    for k, j, xx, cc in peers:
        n = 2 * k + j
        copy = remote(
            m_ref.at[rows(2 * xx + cc)], o_ref.at[:, columns], send.at[n], recv.at[n], {"x": xx, "c": cc}
        )
        copy.start()
        copies.append(copy)
    kept.wait()
    for copy in copies:
        copy.wait()


def to_heads(m, cid):
    return pl.pallas_call(
        to_heads_kernel,
        out_shape=jax.ShapeDtypeStruct((SLOT, LEN), BF),
        in_specs=[pl.BlockSpec(memory_space=pltpu.VMEM)],
        out_specs=pl.BlockSpec(memory_space=pltpu.VMEM),
        scratch_shapes=[pltpu.SemaphoreType.DMA] + [pltpu.SemaphoreType.DMA((8,))] * 2,
        compiler_params=pltpu.CompilerParams(
            collective_id=cid, has_side_effects=True, vmem_limit_bytes=32 << 20
        ),
        name="to_heads",
    )(m)


BLOCK = 256


def dot(a, b, dims):
    return lax.dot_general(a, b, (dims, ((), ())), preferred_element_type=F32)


def attend_kernel(q_ref, k_ref, v_ref, o_ref, p_ref):
    keys = lax.broadcasted_iota(jnp.int32, (BLOCK, BLOCK), 0)
    queries = lax.broadcasted_iota(jnp.int32, (BLOCK, BLOCK), 1)
    for i in range(LEN // BLOCK):
        low, high = i * BLOCK, (i + 1) * BLOCK
        q = q_ref[:, low:high] * BF(HDIM**-0.5)
        parts = [dot(k_ref[:, low:high], q, ((0,), (0,)))]
        parts[0] = jnp.where(keys <= queries, parts[0], MASKED)
        if i:
            parts.insert(0, dot(k_ref[:, :low], q, ((0,), (0,))))
        highest = functools.reduce(jnp.maximum, [jnp.max(s, axis=0, keepdims=True) for s in parts])
        parts = [jnp.exp(s - highest) for s in parts]
        share = 1.0 / sum(jnp.sum(s, axis=0, keepdims=True) for s in parts)
        parts = [(s * share).astype(BF) for s in parts]
        p_ref[0, low:high, low:high] = parts[-1]
        mixed = dot(v_ref[:, low:high], parts[-1], ((1,), (0,)))
        if i:
            p_ref[0, :low, low:high] = parts[0]
            mixed += dot(v_ref[:, :low], parts[0], ((1,), (0,)))
        o_ref[:, low:high] = mixed.astype(BF)


def attend(qkv):
    head = lambda k: pl.BlockSpec((pl.squeezed, HDIM, LEN), lambda h: (k, h, 0))
    return pl.pallas_call(
        attend_kernel,
        grid=(SLOT // HDIM,),
        out_shape=(
            jax.ShapeDtypeStruct((SLOT, LEN), BF),
            jax.ShapeDtypeStruct((SLOT // HDIM, LEN, LEN), BF),
        ),
        in_specs=[head(0), head(1), head(2)],
        out_specs=(
            pl.BlockSpec((HDIM, LEN), lambda h: (h, 0)),
            pl.BlockSpec((1, LEN, LEN), lambda h: (h, 0, 0)),
        ),
        compiler_params=pltpu.CompilerParams(vmem_limit_bytes=40 << 20),
        cost_estimate=pl.CostEstimate(flops=2 * 3 * 2 * 64 * 10 * 65536, bytes_accessed=8 << 20, transcendentals=3 * 655360),
        name="attend",
    )(qkv, qkv, qkv)


def attend_back_kernel(q_ref, k_ref, v_ref, u_ref, p_ref, dq_ref, dk_ref, dv_ref, dk_sum, dv_sum):
    dk_sum[...] = jnp.zeros_like(dk_sum)
    dv_sum[...] = jnp.zeros_like(dv_sum)
    for i in range(LEN // BLOCK):
        low, high = i * BLOCK, (i + 1) * BLOCK
        q = q_ref[:, low:high] * BF(HDIM**-0.5)
        u = u_ref[:, low:high]
        p = p_ref[0, :high, low:high]
        wide = p.astype(F32)
        dp = dot(v_ref[:, :high], u, ((0,), (0,)))
        centre = jnp.sum(wide * dp, axis=0, keepdims=True)
        ds = (wide * (dp - centre)).astype(BF)
        dq_ref[:, low:high] = (dot(k_ref[:, :high], ds, ((1,), (0,))) * HDIM**-0.5).astype(BF)
        dk_sum[:, :high] += dot(q, ds, ((1,), (1,)))
        dv_sum[:, :high] += dot(u, p, ((1,), (1,)))
    dk_ref[...] = dk_sum[...].astype(BF)
    dv_ref[...] = dv_sum[...].astype(BF)


def attend_back(qkv, upstream, probs):
    head = lambda k: pl.BlockSpec((pl.squeezed, HDIM, LEN), lambda h: (k, h, 0))
    flat = pl.BlockSpec((HDIM, LEN), lambda h: (h, 0))
    return pl.pallas_call(
        attend_back_kernel,
        grid=(SLOT // HDIM,),
        out_shape=(jax.ShapeDtypeStruct((SLOT, LEN), BF),) * 3,
        in_specs=[head(0), head(1), head(2), flat, pl.BlockSpec((1, LEN, LEN), lambda h: (h, 0, 0))],
        out_specs=(flat,) * 3,
        scratch_shapes=[pltpu.VMEM((HDIM, LEN), F32)] * 2,
        compiler_params=pltpu.CompilerParams(vmem_limit_bytes=40 << 20),
        cost_estimate=pl.CostEstimate(flops=4 * 3 * 2 * 64 * 10 * 65536, bytes_accessed=8 << 20, transcendentals=0),
        name="attend_back",
    )(qkv, qkv, qkv, upstream, probs)


def swap(a, axis):
    return lax.ppermute(a, axis, [(0, 1), (1, 0)])


def shifted(a, axis, k):
    return lax.ppermute(a, axis, [(i, (i + k) % 4) for i in range(4)])


def pick(flag, a, b):
    return jnp.where(flag, a, b), jnp.where(flag, b, a)


def at(a, i):
    return lax.dynamic_index_in_dim(a, i, 0, keepdims=False)


def halves(c, mine, theirs):
    first, second = pick(c == 0, mine, theirs)
    return jnp.concatenate([first, second], axis=-1)


def tokens_in(a, zh, c):
    mine, other = at(a, zh), at(a, 1 - zh)
    got = swap(other, "zh")
    keep, send = pick(zh == c, mine, got)
    return halves(c, keep, swap(send, "c"))


def tokens_out(a, zh, c):
    keep, send = pick(c == 0, a[:, :HALF], a[:, HALF:])
    part, other = pick(c == zh, keep, swap(send, "c"))
    got = swap(other, "zh")
    first, second = pick(zh == 0, part, got)
    return jnp.stack([first, second])


def weight_in(w, zh, c):
    keep, send = pick(zh == c, w, swap(w, "zh"))
    return halves(c, keep, swap(send, "c"))


def over_replicas(pieces):
    y = lax.axis_index("y")
    pieces = pieces.astype(BF)
    total = at(pieces, y).astype(F32)
    for k in (2, 1, 3):
        total += shifted(at(pieces, lax.rem(y + k, 4)), "y", k).astype(F32)
    total = total.astype(BF)
    total = (total.astype(F32) + swap(total, "zl").astype(F32)).astype(BF)
    found = jnp.stack([total] + [shifted(total, "y", 4 - k) for k in (1, 2, 3)])
    return jnp.concatenate([at(found, lax.rem(k - y + 4, 4))[None] for k in range(4)])


def block_grad(grad, zh, c):
    rows = grad.shape[0]
    keep, send = pick(c == 0, grad[:, :HALF], grad[:, HALF:])
    block, other = pick(c == zh, keep, swap(send, "c"))
    total = block.astype(F32) + swap(other, "zh").astype(F32)
    return over_replicas(total.reshape(4, rows // 4, HALF)).reshape(rows, HALF).astype(F32)


def normed(values, gain, shift):
    centre = jnp.mean(values, axis=1, keepdims=True)
    second = jnp.mean(values * values, axis=1, keepdims=True)
    inverse = lax.rsqrt(second - centre * centre + EPSILON)
    centred = (values - centre) * inverse
    return (centred * gain + shift).astype(BF), centred, inverse


def normed_back(upstream, centred, inverse, gain):
    scaled = upstream * gain
    result = inverse * (
        scaled
        - jnp.mean(scaled, axis=1, keepdims=True)
        - centred * jnp.mean(scaled * centred, axis=1, keepdims=True)
    )
    return result, jnp.sum(upstream * centred, axis=0), jnp.sum(upstream, axis=0)


def per_device(
    block_in,
    query_key_value_weight,
    bias_qv,
    output_weight,
    bias_out,
    gain_one,
    shift_one,
    gain_two,
    shift_two,
    up_weight,
    bias_up,
    down_weight,
    bias_down,
    out_grad,
):
    x, y, zh, c = (lax.axis_index(a) for a in ("x", "y", "zh", "c"))
    rank = 2 * x + c
    last = rank == 7

    inputs = tokens_in(block_in, zh, c).astype(F32)
    columns = jnp.stack([bias_out, gain_one, shift_one, gain_two, shift_two, bias_down])
    bias_out, gain_one, shift_one, gain_two, shift_two, bias_down = halves(c, columns, swap(columns, "c"))

    w = query_key_value_weight
    even, odd = pick(zh == 0, w, swap(w, "zh"))
    w = jnp.concatenate([even, odd], axis=1)
    w = jnp.concatenate([shifted(w[:, 224:], "x", 1), w, jnp.zeros((3, 48, HALF), BF)], axis=1)
    mine = lax.dynamic_slice_in_dim(w, 48 - 16 * x + 128 * c, SLOT, 1)
    theirs = lax.dynamic_slice_in_dim(w, 48 - 16 * x + 128 * (1 - c), SLOT, 1)
    weight_qkv = halves(c, mine, swap(theirs, "c"))
    real = jnp.logical_or(jnp.arange(SLOT) < 128, last)
    weight_qkv = jnp.where(real[None, :, None], weight_qkv, BF(0))

    rows = jnp.concatenate([bias_qv.reshape(-1), bias_up])
    even, odd = pick(zh == 0, rows, swap(rows, "zh"))
    bias_up = jnp.where(c == 0, even[272:], odd[272:])
    qv = jnp.concatenate([even[:272].reshape(2, 136), odd[:272].reshape(2, 136)], axis=1)
    qv = jnp.concatenate([shifted(qv[:, 224:], "x", 1), qv, jnp.zeros((2, 48), F32)], axis=1)
    qv = lax.dynamic_slice_in_dim(qv, 48 - 16 * x + 128 * c, SLOT, 1)
    qv = jnp.where(real[None], qv, 0.0)
    bias_qkv = jnp.stack([qv[0], jnp.zeros_like(qv[0]), qv[1]])

    normed_one, centred_one, inverse_one = normed(inputs, gain_one, shift_one)
    first_rows = line_gather(normed_one, 1).reshape(LEN, D)
    qkv = jnp.einsum("koi,ti->kot", weight_qkv, first_rows, preferred_element_type=F32)
    qkv = (qkv + bias_qkv[..., None]).astype(BF)
    mixed, probs = attend(qkv)
    found = to_tokens(mixed, 2)
    mixed_here = jnp.concatenate([found[:7, :128].reshape(896, TOK), found[7]])

    even, odd = pick(zh == 0, output_weight, swap(output_weight, "zh"))
    wo = jnp.concatenate([even, odd]).reshape(4, 68, HALF)
    part = at(wo, y)
    parts = jnp.stack([part] + [shifted(part, "x", 4 - k) for k in (1, 2, 3)])
    parts = jnp.concatenate([at(parts, lax.rem(k - x + 4, 4))[None] for k in range(4)])
    parts = jnp.stack([parts] + [shifted(parts, "y", 4 - k) for k in (1, 2, 3)])
    parts = jnp.concatenate([at(parts, lax.rem(k - y + 4, 4))[None] for k in range(4)])
    wo = jnp.transpose(parts, (1, 0, 2, 3)).reshape(D, HALF)
    wo = halves(c, wo, swap(wo, "c"))

    attended = jnp.einsum("ft,fo->to", mixed_here, wo, preferred_element_type=F32) + bias_out
    residual = inputs + attended

    weight_up = weight_in(up_weight, zh, c)
    weight_down = weight_in(down_weight, zh, c)
    normed_two, centred_two, inverse_two = normed(residual, gain_two, shift_two)
    second_rows = line_gather(normed_two, 3).reshape(LEN, D)
    hidden = jnp.einsum("td,fd->tf", second_rows, weight_up, preferred_element_type=F32) + bias_up
    cumulative = 0.5 * (1.0 + lax.erf(hidden * 0.7071067811865476))
    density = jnp.exp(-0.5 * hidden * hidden) * 0.3989422804014327
    active = (hidden * cumulative).astype(BF)
    slope = cumulative + hidden * density
    lowered = jnp.einsum("tf,fo->to", active, weight_down, preferred_element_type=F32).astype(BF)
    lowered = line_scatter(lowered.reshape(8, TOK, D), 4)
    block_out = tokens_out((residual + (lowered + bias_down)).astype(BF), zh, c)

    tangent = tokens_in(out_grad, zh, c)
    tangent_rows = line_gather(tangent, 5).reshape(LEN, D)
    down_grad = jnp.einsum("tf,to->fo", active, tangent_rows, preferred_element_type=F32).astype(BF)
    down_weight_gradient = block_grad(down_grad, zh, c)
    d_active = jnp.einsum("to,fo->tf", tangent_rows, weight_down, preferred_element_type=F32)
    d_hidden = (d_active * slope).astype(BF)
    grad_bias_up = jnp.sum(d_hidden, axis=0, dtype=F32)
    up_grad = jnp.einsum("tf,to->fo", d_hidden, second_rows, preferred_element_type=F32).astype(BF)
    up_weight_gradient = block_grad(up_grad, zh, c)
    d_normed_two = jnp.einsum("tf,fd->td", d_hidden, weight_up, preferred_element_type=F32).astype(BF)
    d_normed_two = line_scatter(d_normed_two.reshape(8, TOK, D), 6)
    tangent = tangent.astype(F32)
    grad_bias_down = jnp.sum(tangent, axis=0)
    part, grad_gain_two, grad_shift_two = normed_back(d_normed_two, centred_two, inverse_two, gain_two)
    d_residual = tangent + part
    d_attended = d_residual.astype(BF)
    grad_bias_out = jnp.sum(d_attended, axis=0, dtype=F32)

    d_mixed = jnp.einsum("fo,to->ft", wo, d_attended, preferred_element_type=F32).astype(BF)
    upstream = to_heads(d_mixed, 7)
    grad_out = jnp.einsum("ft,to->fo", mixed_here, d_attended, preferred_element_type=F32).astype(BF)
    keep, send = pick(c == 0, grad_out[:, :HALF], grad_out[:, HALF:])
    grad_out = (keep.astype(F32) + swap(send, "c").astype(F32)).astype(BF).reshape(4, 272, HALF)
    total = at(grad_out, x).astype(F32)
    for k in (2, 1, 3):
        total += shifted(at(grad_out, lax.rem(x + k, 4)), "x", k).astype(F32)
    keep, send = pick(zh == 0, total[:136], total[136:])
    grad_out = keep + swap(send.astype(BF), "zh").astype(F32)
    grad_out = over_replicas(grad_out.reshape(4, 34, HALF)).reshape(136, HALF).astype(F32)

    d_query, d_key, d_value = attend_back(qkv, upstream, probs)
    d_qkv = jnp.stack([d_query, d_key, d_value])
    d_normed_one = jnp.einsum("kot,koi->ti", d_qkv, weight_qkv, preferred_element_type=F32).astype(BF)
    d_normed_one = line_scatter(d_normed_one.reshape(8, TOK, D), 8)
    grad_qkv = jnp.einsum("kot,ti->koi", d_qkv, first_rows, preferred_element_type=F32).astype(BF)
    keep, send = pick(c == 0, grad_qkv[..., :HALF], grad_qkv[..., HALF:])
    first, second = pick(c == 0, keep, swap(send, "c"))
    tail = jnp.pad(shifted(first[:, :48], "x", 3), ((0, 0), (0, 16), (0, 0)))
    chip = jnp.concatenate([first[:, :128], second[:, :128], jnp.where(x == 3, second[:, 128:], tail)], axis=1)
    chip = lax.dynamic_slice_in_dim(chip, 16 * x, 272, 1)
    keep, send = pick(zh == 0, chip[:, :136], chip[:, 136:])
    total = keep.astype(F32) + swap(send, "zh").astype(F32)
    grad_qkv = over_replicas(total.reshape(4, 102, HALF)).reshape(3, 136, HALF).astype(F32)

    part, grad_gain_one, grad_shift_one = normed_back(d_normed_one, centred_one, inverse_one, gain_one)
    in_grad = tokens_out((d_residual + part).astype(BF), zh, c).astype(F32)

    bias_sums = jnp.sum(d_qkv, axis=2, dtype=F32)
    bias_sums = jnp.where(real[None], jnp.stack([bias_sums[0], bias_sums[2]]), 0.0)
    wide = lax.dynamic_update_slice(jnp.zeros((2, D), F32), bias_sums, (0, 128 * rank))
    hidden_sums = lax.dynamic_update_slice(jnp.zeros((8, 544), F32), grad_bias_up[None], (rank, 0))
    vector = jnp.concatenate(
        [grad_bias_out, grad_gain_one, grad_shift_one, grad_gain_two, grad_shift_two, grad_bias_down]
        + [wide.reshape(-1), hidden_sums.reshape(-1)]
    )
    vector = lax.psum(vector, ALL)
    six = vector[: 6 * D].reshape(6, 2, HALF)
    grad_bias_out, grad_gain_one, grad_shift_one, grad_gain_two, grad_shift_two, grad_bias_down = (
        lax.dynamic_index_in_dim(six, c, 1, keepdims=False)
    )
    row = 2 * x + zh
    grad_bias_qv = lax.dynamic_slice(vector[6 * D : 8 * D].reshape(2, D), (0, 136 * row), (2, 136))
    grad_bias_up = lax.dynamic_slice_in_dim(vector[8 * D :], 544 * row, 544, 0)

    return (
        block_out,
        in_grad,
        grad_qkv,
        grad_bias_qv,
        grad_out,
        grad_bias_out,
        grad_gain_one,
        grad_shift_one,
        grad_gain_two,
        grad_shift_two,
        up_weight_gradient,
        grad_bias_up,
        down_weight_gradient,
        grad_bias_down,
    )


def solution(mesh):
    finer = Mesh(mesh.devices.reshape(2, 4, 4, 2, 2), ALL)
    return jax.shard_map(
        per_device,
        mesh=finer,
        in_specs=(
            P(DP, ROW, "c"),
            P(None, ROW, "c"),
            P(None, ROW),
            P(ROW, "c"),
            P("c"),
            P("c"),
            P("c"),
            P("c"),
            P("c"),
            P(ROW, "c"),
            P(ROW),
            P(ROW, "c"),
            P("c"),
            P(DP, ROW, "c"),
        ),
        out_specs=(
            P(DP, ROW, "c"),
            P(DP, ROW, "c"),
            P(None, ROW, "c"),
            P(None, ROW),
            P(ROW, "c"),
            P("c"),
            P("c"),
            P("c"),
            P("c"),
            P("c"),
            P(ROW, "c"),
            P(ROW),
            P(ROW, "c"),
            P("c"),
        ),
        check_vma=False,
    )
```

time: 1230 us -> 498 us (0.40)
  waiting for transfers between devices: 553 us -> 74.8 us
  matrix products: 197 us -> 31 us
  Pallas kernels: 0 us -> 143 us
  blocking collectives: 150 us -> 67.1 us
  local copies, waits for them, and re-layouts: 110 us -> 47.1 us
  loops' own time: 55.7 us -> 0 us
  other arithmetic: 85.1 us -> 46 us
  starting transfers between devices: 46.6 us -> 77.4 us
    reduce_scatter x9 -> x0, waiting for transfers between devices: 335 us -> none  [the longest x8 240 us: scatter_axes(): nearer = lax.psum_scatter(x, axes[0], scatter_dimension=dim, tiled=True)]
    dot_general x131 -> x12, matrix products: 197 us -> 31 us  [the longest x1 3.63 us: per_device(): jnp.einsum('kot,koi->ti', d_qkv, weight_qkv, preferred_element_type=F32)]
    pallas_call x0 -> x10, Pallas kernels: none -> 143 us  [the longest x3 57.2 us: line_scatter(): pl.pallas_call(scatter_kernel, out_shape=jax.ShapeDtypeStruct(p.shape[1:]...]
    all_to_all x10 -> x0, blocking collectives: 101 us -> none  [the longest x5 53 us: sent_to_all(): lax.all_to_all(jnp.broadcast_to(x[None], (size, *x.shape)), axis, 0, 0, t...]
    psum x1 -> x0, waiting for transfers between devices: 90.2 us -> none  [per_device(): lax.psum((grad_qkv, grad_bias_qv, grad_out, grad_bias_out, up_weight_grad...]
    ppermute x0 -> x66, starting transfers between devices: none -> 77.4 us  [the longest x36 46.9 us: shifted(): return lax.ppermute(a, axis, [(i, (i + k) % 4) for i in range(4)])]
    all_to_all x7 -> x0, waiting for transfers between devices: 77.1 us -> none  [the longest x4 61.6 us: sent_to_all(): lax.all_to_all(jnp.broadcast_to(x[None], (size, *x.shape)), axis, 0, 0, t...]
    ppermute x0 -> x66, waiting for transfers between devices: none -> 74.8 us  [the longest x30 52.5 us: swap(): return lax.ppermute(a, axis, [(0, 1), (1, 0)])]
  transfers between devices with their start and end apart: 18 -> 66, of which waited for: 14 -> 23; matrix products, arithmetic and copies ran while one was open for 6% -> 14% of each run, Pallas kernels for 0% -> 10%
where the time goes in v1:
time: 498 us; the launch traced here: 490 us
  Pallas kernels  143 us (29%)
  starting transfers between devices  77.4 us (16%)
  waiting for transfers between devices  74.8 us (15%)
  blocking collectives  67.1 us (13%)
  local copies, waits for them, and re-layouts  47.1 us (9%)
  other arithmetic  46 us (9%)
  matrix products  31 us (6%)
    psum x1, blocking collectives, per_device(): vector = lax.psum(vector, ALL)  67.1 us
    pallas_call x3, Pallas kernels, line_scatter(): pl.pallas_call(scatter_kernel, out_shape=jax.ShapeDtypeStruct(p.shape[1:]...  57.2 us
    pallas_call x3, Pallas kernels, line_gather(): pl.pallas_call(gather_kernel, out_shape=jax.ShapeDtypeStruct((8, *a.shape...  54.9 us
    ppermute x30, waiting for transfers between devices, swap(): return lax.ppermute(a, axis, [(0, 1), (1, 0)])  52.5 us
    ppermute x36, starting transfers between devices, shifted(): return lax.ppermute(a, axis, [(i, (i + k) % 4) for i in range(4)])  46.9 us
    ppermute x30, starting transfers between devices, swap(): return lax.ppermute(a, axis, [(0, 1), (1, 0)])  30.6 us
    ppermute x36, waiting for transfers between devices, shifted(): return lax.ppermute(a, axis, [(i, (i + k) % 4) for i in range(4)])  22.3 us
    select_n x26, other arithmetic, pick(): return (jnp.where(flag, a, b), jnp.where(flag, b, a))  19.7 us
  transfers between devices with their start and end apart: 66, of which 23 were waited for; matrix products, arithmetic and copies ran while one was open for 14% of the time, Pallas kernels for 10%

profile of v1, /device:TPU:6, one launch (start us, length us, event | category | flops | bytes accessed | tf_op | source)
XLA Modules:
  0.0 489.7 jit_solution(560848281676725252)
XLA Ops:
  2.3 3.9 collective-permute-start.6
  11.7 3.6 collective-permute-start
  21.7 3.4 collective-permute-start.2
  31.6 3.2 collective-permute-done.10
  36.0 3.3 collective-permute-start.13
  42.7 16.9 %line_gather.3 = bf16[8,128,1088]{2,1,0:T(8,128)(2,1)S(1)} custom-call(bf16[128,1088]{1,0:T(8,128)(2,1)S(1)} %fusion.18.a_ref), custom_call_target="tpu_custom_call" | custom-call | tf_op jit(solution)/shard_map/line_gather/pallas_call | solution.py:68
  59.6 19.2 %line_gather.5 = bf16[8,128,1088]{2,1,0:T(8,128)(2,1)S(1)} custom-call(bf16[128,1088]{1,0:T(8,128)(2,1)S(1)} %get-tuple-element.77.a_ref), custom_call_target="tpu_custom_call" | custom-call | tf_op jit(solution)/shard_map/line_gather/pallas_call | solution.py:68
  78.9 3.5 collective-permute-start.18
  88.4 10.1 %collective-permute-done.18 = bf16[544,544]{1,0:T(8,128)(2,1)S(1)} collective-permute-done((bf16[544,544]{1,0:T(8,128)(2,1)S(1)}, bf16[544,544]{1,0:T(8,128)(2,1)S(1)}, u32[]{:S(2)}, u32[]{:S(2)}) %collective-permute-start.18) | collective-permute-done | bytes 591904 | tf_op jit(solution)/shard_map/ppermute | solution.py:286
  104.1 4.4 copy.72
  108.5 6.3 %reshape.240 = bf16[1088,544]{0,1:T(8,128)(2,1)} reshape(bf16[4,4,68,544]{2,1,0,3:T(4,128)(2,1)} %copy.72) | data formatting | bytes 2367488 | tf_op jit(solution)/shard_map/reshape | solution.py:422
  121.0 6.1 %attend.1 = (bf16[192,1024]{1,0:T(8,128)(2,1)S(1)}, bf16[3,1024,1024]{2,1,0:T(8,128)(2,1)S(1)}) custom-call(bf16[3,192,1024]{2,1,0:T(8,128)(2,1)S(1)} %add_convert_fusion.1.q_ref.k_ref.v_ref, bf16[3,192,1024]{2,1,0:T(8,128)(2,1)S(1)} %add_convert_fusion.1.q_ref.k_ref.v_ref, bf16[3,192,1024]{2,1,0:T(8,128)(2,1)S(1)} %add_convert_fusion.1.q_ref.k_ref.v_ref), custom_call_target="tpu_custom_call" | custom-call | flops 503316480 | bytes 8388608 | tf_op jit(solution)/shard_map/attend/pallas_call | solution.py:232
  127.1 8.6 %to_tokens.1 = bf16[8,192,128]{2,1,0:T(8,128)(2,1)S(1)} custom-call(bf16[192,1024]{1,0:T(8,128)(2,1)S(1)} %get-tuple-element.19.m_ref), custom_call_target="tpu_custom_call" | custom-call | tf_op jit(solution)/shard_map/to_tokens/pallas_call | solution.py:149
  139.0 18.9 %line_gather.4 = bf16[8,128,1088]{2,1,0:T(8,128)(2,1)S(1)} custom-call(bf16[128,1088]{1,0:T(8,128)(2,1)S(1)} %add_convert_fusion.6.a_ref), custom_call_target="tpu_custom_call" | custom-call | tf_op jit(solution)/shard_map/line_gather/pallas_call | solution.py:68
  162.4 3.6 convolution_convert_fusion.2
  171.6 3.5 convolution_convert_fusion.1
  178.1 19.0 %line_scatter.3 = f32[128,1088]{1,0:T(8,128)S(1)} custom-call(bf16[8,128,1088]{2,1,0:T(8,128)(2,1)S(1)} %bitcast.136), custom_call_target="tpu_custom_call" | custom-call | tf_op jit(solution)/shard_map/line_scatter/pallas_call | solution.py:111
  201.2 19.0 %line_scatter.4 = f32[128,1088]{1,0:T(8,128)S(1)} custom-call(bf16[8,128,1088]{2,1,0:T(8,128)(2,1)S(1)} %bitcast.137), custom_call_target="tpu_custom_call" | custom-call | tf_op jit(solution)/shard_map/line_scatter/pallas_call | solution.py:111
  226.3 8.5 %to_heads.1.u_ref = bf16[192,1024]{1,0:T(8,128)(2,1)S(1)} custom-call(bf16[1088,128]{1,0:T(8,128)(2,1)S(1)} %convolution_convert_fusion.6.m_ref), custom_call_target="tpu_custom_call" | custom-call | tf_op jit(solution)/shard_map/to_heads/pallas_call | solution.py:188
  234.8 8.2 %attend_back.1 = (bf16[192,1024]{1,0:T(8,128)(2,1)S(1)}, bf16[192,1024]{1,0:T(8,128)(2,1)S(1)}, bf16[192,1024]{1,0:T(8,128)(2,1)S(1)}) custom-call(bf16[3,192,1024]{2,1,0:T(8,128)(2,1)S(1)} %add_convert_fusion.1.q_ref.k_ref.v_ref, bf16[3,192,1024]{2,1,0:T(8,128)(2,1)S(1)} %add_convert_fusion.1.q_ref.k_ref.v_ref, ...), custom_call_target="tpu_custom_call" | custom-call | flops 1006632960 | bytes 8388608 | tf_op jit(solution)/shard_map/attend_back/pallas_call | solution.py:272
  246.0 3.6 bitcast_convert_fusion
  253.2 19.1 %line_scatter.5 = f32[128,1088]{1,0:T(8,128)S(1)} custom-call(bf16[8,128,1088]{2,1,0:T(8,128)(2,1)S(1)} %bitcast.138), custom_call_target="tpu_custom_call" | custom-call | tf_op jit(solution)/shard_map/line_scatter/pallas_call | solution.py:111
  273.3 67.1 %psum.7 = f32[13056]{0:T(1024)S(1)} all-reduce(f32[13056]{0:T(1024)S(1)} %concatenate.76), channel_id=1, replica_groups=mesh['zl'=2,'y'=4,'x'=4,'zh'=2,'c'=2] {'zl','y','x','zh','c'}, use_global_device_ids=true, to_apply=%region_16.17 | all-reduce | flops 13056 | bytes 104448 | tf_op jit(solution)/shard_map/psum | solution.py:496
  354.7 6.3 %collective-permute-done.25 = bf16[128,544]{1,0:T(8,128)(2,1)S(1)} collective-permute-done((bf16[128,544]{1,0:T(8,128)(2,1)S(1)}, bf16[128,544]{1,0:T(8,128)(2,1)S(1)}, u32[]{:S(2)}, u32[]{:S(2)}) %collective-permute-start.25) | collective-permute-done | bytes 139296 | tf_op jit(solution)/shard_map/ppermute | solution.py:286
  362.4 5.4 %collective-permute-done.21 = bf16[128,544]{1,0:T(8,128)(2,1)S(1)} collective-permute-done((bf16[128,544]{1,0:T(8,128)(2,1)S(1)}, bf16[128,544]{1,0:T(8,128)(2,1)S(1)}, u32[]{:S(2)}, u32[]{:S(2)}) %collective-permute-start.21) | collective-permute-done | bytes 139296 | tf_op jit(solution)/shard_map/ppermute | solution.py:286
  377.5 3.8 collective-permute-done.27
  385.5 6.4 %collective-permute-done.58 = bf16[544,544]{1,0:T(8,128)(2,1)S(1)} collective-permute-done((bf16[544,544]{1,0:T(8,128)(2,1)S(1)}, bf16[544,544]{1,0:T(8,128)(2,1)S(1)}, u32[]{:S(2)}, u32[]{:S(2)}) %collective-permute-start.58) | collective-permute-done | bytes 591904 | tf_op jit(solution)/shard_map/ppermute | solution.py:286
  395.9 11.0 %collective-permute-done.49 = bf16[544,544]{1,0:T(8,128)(2,1)S(1)} collective-permute-done((bf16[544,544]{1,0:T(8,128)(2,1)S(1)}, bf16[544,544]{1,0:T(8,128)(2,1)S(1)}, u32[]{:S(2)}, u32[]{:S(2)}) %collective-permute-start.49) | collective-permute-done | bytes 591904 | tf_op jit(solution)/shard_map/ppermute | solution.py:286
  437.1 3.6 collective-permute-done.32
  442.2 4.1 collective-permute-done.53
  473.8 3.4 collective-permute-done.42
  477.5 4.0 collective-permute-done.44
  (427 shorter events, 175.9 us)
Async XLA Ops:
  2.3 15.6 %collective-permute-start.6 = (f32[816]{0:T(1024)S(1)}, f32[816]{0:T(1024)S(1)}, u32[]{:S(2)}, u32[]{:S(2)}) collective-permute-start(f32[816]{0:T(1024)S(1)} %pad_maximum_fusion.27), channel_id=1, source_target_pairs={{0,2},{2,0},{1,3},{3,1},{4,6},{6,4},{5,7},{7,5},{8,10},{10,8},{9,1... | collective-permute-start | bytes 9800 | tf_op jit(solution)/shard_map/ppermute | solution.py:286
  10.3 15.5 %collective-permute-start.5 = (f32[6,544]{1,0:T(8,128)S(1)}, f32[6,544]{1,0:T(8,128)S(1)}, u32[]{:S(2)}, u32[]{:S(2)}) collective-permute-start(f32[6,544]{1,0:T(8,128)S(1)} %stack.151), channel_id=1, source_target_pairs={{0,1},{1,0},{2,3},{3,2},{4,5},{5,4},{6,7},{7,6},{8,9},{9,8},{10,11... | collective-permute-start | bytes 39176 | tf_op jit(solution)/shard_map/ppermute | solution.py:286
  10.4 16.4 %collective-permute-start.8 = (bf16[136,544]{1,0:T(8,128)(2,1)}, bf16[136,544]{1,0:T(8,128)(2,1)S(1)}, u32[]{:S(2)}, u32[]{:S(2)}) collective-permute-start(bf16[136,544]{1,0:T(8,128)(2,1)} %param.17), channel_id=1, source_target_pairs={{0,2},{2,0},{1,3},{3,1},{4,6},{6,4},{5,7},{7,5},{8,10},{10,8},{9,1... | collective-permute-start | bytes 443912 | tf_op jit(solution)/shard_map/ppermute | solution.py:286
  11.7 15.0 %collective-permute-start = (bf16[128,544]{1,0:T(8,128)(2,1)S(1)}, bf16[128,544]{1,0:T(8,128)(2,1)S(1)}, u32[]{:S(2)}, u32[]{:S(2)}) collective-permute-start(bf16[128,544]{1,0:T(8,128)(2,1)S(1)} %bitcast.176), channel_id=1, source_target_pairs={{0,2},{2,0},{1,3},{3,1},{4,6},{6,4},{5,7},{7,5},{8,10},{10,8},{9,1... | collective-permute-start | bytes 417800 | tf_op jit(solution)/shard_map/ppermute | solution.py:286
  16.4 10.3 %collective-permute-start.22 = (bf16[128,544]{1,0:T(8,128)(2,1)S(1)}, bf16[128,544]{1,0:T(8,128)(2,1)S(1)}, u32[]{:S(2)}, u32[]{:S(2)}) collective-permute-start(bf16[128,544]{1,0:T(8,128)(2,1)S(1)} %bitcast.177), channel_id=1, source_target_pairs={{0,2},{2,0},{1,3},{3,1},{4,6},{6,4},{5,7},{7,5},{8,10},{10,8},{9,1... | collective-permute-start | bytes 417800 | tf_op jit(solution)/shard_map/ppermute | solution.py:286
  21.7 57.2 %collective-permute-start.2 = (bf16[3,136,544]{2,1,0:T(8,128)(2,1)}, bf16[3,136,544]{2,1,0:T(8,128)(2,1)}, u32[]{:S(2)}, u32[]{:S(2)}) collective-permute-start(bf16[3,136,544]{2,1,0:T(8,128)(2,1)} %param.15), channel_id=1, source_target_pairs={{0,2},{2,0},{1,3},{3,1},{4,6},{6,4},{5,7},{7,5},{8,10},{10,8},{9,1... | collective-permute-start | bytes 1331720 | tf_op jit(solution)/shard_map/ppermute | solution.py:286
  25.8 60.5 %collective-permute-start.16 = (bf16[544,544]{1,0:T(8,128)(2,1)S(1)}, bf16[544,544]{1,0:T(8,128)(2,1)}, u32[]{:S(2)}, u32[]{:S(2)}) collective-permute-start(bf16[544,544]{1,0:T(8,128)(2,1)S(1)} %copy-done.29), channel_id=1, source_target_pairs={{0,2},{2,0},{1,3},{3,1},{4,6},{6,4},{5,7},{7,5},{8,10},{10,8},{9,1... | collective-permute-start | bytes 1775624 | tf_op jit(solution)/shard_map/ppermute | solution.py:286
  36.0 47.7 %collective-permute-start.13 = (bf16[4,68,544]{2,1,0:T(8,128)(2,1)S(1)}, bf16[4,68,544]{2,1,0:T(8,128)(2,1)S(1)}, u32[]{:S(2)}, u32[]{:S(2)}) collective-permute-start(bf16[4,68,544]{2,1,0:T(8,128)(2,1)S(1)} %get-tuple-element.134), channel_id=1, source_target_pairs={{0,32},{16,48},{32,0},{48,16},{1,33},{17,49},{33,1},{49,17},{2,34}... | collective-permute-start | bytes 887816 | tf_op jit(solution)/shard_map/ppermute | solution.py:290
  39.3 46.5 %collective-permute-start.12 = (bf16[4,68,544]{2,1,0:T(8,128)(2,1)S(1)}, bf16[4,68,544]{2,1,0:T(8,128)(2,1)S(1)}, u32[]{:S(2)}, u32[]{:S(2)}) collective-permute-start(bf16[4,68,544]{2,1,0:T(8,128)(2,1)S(1)} %get-tuple-element.134), channel_id=1, source_target_pairs={{0,48},{16,0},{32,16},{48,32},{1,49},{17,1},{33,17},{49,33},{2,50}... | collective-permute-start | bytes 887816 | tf_op jit(solution)/shard_map/ppermute | solution.py:290
  40.9 45.0 %collective-permute-start.14 = (bf16[4,68,544]{2,1,0:T(8,128)(2,1)S(1)}, bf16[4,68,544]{2,1,0:T(8,128)(2,1)S(1)}, u32[]{:S(2)}, u32[]{:S(2)}) collective-permute-start(bf16[4,68,544]{2,1,0:T(8,128)(2,1)S(1)} %get-tuple-element.134), channel_id=1, source_target_pairs={{0,16},{16,32},{32,48},{48,0},{1,17},{17,33},{33,49},{49,1},{2,18}... | collective-permute-start | bytes 887816 | tf_op jit(solution)/shard_map/ppermute | solution.py:290
  78.9 19.6 %collective-permute-start.18 = (bf16[544,544]{1,0:T(8,128)(2,1)S(1)}, bf16[544,544]{1,0:T(8,128)(2,1)S(1)}, u32[]{:S(2)}, u32[]{:S(2)}) collective-permute-start(bf16[544,544]{1,0:T(8,128)(2,1)S(1)} %copy-done.30), channel_id=1, source_target_pairs={{0,2},{2,0},{1,3},{3,1},{4,6},{6,4},{5,7},{7,5},{8,10},{10,8},{9,1... | collective-permute-start | bytes 1775624 | tf_op jit(solution)/shard_map/ppermute | solution.py:286
  83.7 15.9 %collective-permute-start.3 = (bf16[3,48,544]{2,1,0:T(8,128)(2,1)S(1)}, bf16[3,48,544]{2,1,0:T(8,128)(2,1)S(1)}, u32[]{:S(2)}, u32[]{:S(2)}) collective-permute-start(bf16[3,48,544]{2,1,0:T(8,128)(2,1)S(1)} %slice.184), channel_id=1, source_target_pairs={{0,4},{4,8},{8,12},{12,0},{1,5},{5,9},{9,13},{13,1},{2,6},{6,10},{... | collective-permute-start | bytes 470024 | tf_op jit(solution)/shard_map/ppermute | solution.py:290
  88.4 26.4 %collective-permute-start.17 = (bf16[544,544]{1,0:T(8,128)(2,1)}, bf16[544,544]{1,0:T(8,128)(2,1)}, u32[]{:S(2)}, u32[]{:S(2)}) collective-permute-start(bf16[544,544]{1,0:T(8,128)(2,1)} %broadcast_select_fusion.13), channel_id=1, source_target_pairs={{0,1},{1,0},{2,3},{3,2},{4,5},{5,4},{6,7},{7,6},{8,9},{9,8},{10,11... | collective-permute-start | bytes 1775624 | tf_op jit(solution)/shard_map/ppermute | solution.py:286
  99.6 16.6 %collective-permute-start.19 = (bf16[544,544]{1,0:T(8,128)(2,1)}, bf16[544,544]{1,0:T(8,128)(2,1)}, u32[]{:S(2)}, u32[]{:S(2)}) collective-permute-start(bf16[544,544]{1,0:T(8,128)(2,1)} %broadcast_select_fusion.11), channel_id=1, source_target_pairs={{0,1},{1,0},{2,3},{3,2},{4,5},{5,4},{6,7},{7,6},{8,9},{9,8},{10,11... | collective-permute-start | bytes 1775624 | tf_op jit(solution)/shard_map/ppermute | solution.py:286
  102.0 15.7 %collective-permute-start.4 = (bf16[3,192,544]{2,1,0:T(8,128)(2,1)}, bf16[3,192,544]{2,1,0:T(8,128)(2,1)}, u32[]{:S(2)}, u32[]{:S(2)}) collective-permute-start(bf16[3,192,544]{2,1,0:T(8,128)(2,1)} %constant_dynamic-slice_fusion.37), channel_id=1, source_target_pairs={{0,1},{1,0},{2,3},{3,2},{4,5},{5,4},{6,7},{7,6},{8,9},{9,8},{10,11... | collective-permute-start | bytes 1880072 | tf_op jit(solution)/shard_map/ppermute | solution.py:286
  114.8 21.0 %collective-permute-start.15 = (bf16[1088,544]{0,1:T(8,128)(2,1)}, bf16[1088,544]{0,1:T(8,128)(2,1)S(1)}, u32[]{:S(2)}, u32[]{:S(2)}) collective-permute-start(bf16[1088,544]{0,1:T(8,128)(2,1)} %reshape.240), channel_id=1, source_target_pairs={{0,1},{1,0},{2,3},{3,2},{4,5},{5,4},{6,7},{7,6},{8,9},{9,8},{10,11... | collective-permute-start | bytes 3551240 | tf_op jit(solution)/shard_map/ppermute | solution.py:286
  345.2 24.7 %collective-permute-start.57 = (bf16[544,544]{1,0:T(8,128)(2,1)}, bf16[544,544]{1,0:T(8,128)(2,1)}, u32[]{:S(2)}, u32[]{:S(2)}) collective-permute-start(bf16[544,544]{1,0:T(8,128)(2,1)} %broadcast_select_fusion.15), channel_id=1, source_target_pairs={{0,1},{1,0},{2,3},{3,2},{4,5},{5,4},{6,7},{7,6},{8,9},{9,8},{10,11... | collective-permute-start | bytes 1775624 | tf_op jit(solution)/shard_map/ppermute | solution.py:286
  345.2 29.5 %collective-permute-start.48 = (bf16[544,544]{1,0:T(8,128)(2,1)}, bf16[544,544]{1,0:T(8,128)(2,1)}, u32[]{:S(2)}, u32[]{:S(2)}) collective-permute-start(bf16[544,544]{1,0:T(8,128)(2,1)} %broadcast_select_fusion.17), channel_id=1, source_target_pairs={{0,1},{1,0},{2,3},{3,2},{4,5},{5,4},{6,7},{7,6},{8,9},{9,8},{10,11... | collective-permute-start | bytes 1775624 | tf_op jit(solution)/shard_map/ppermute | solution.py:286
  349.4 23.6 %collective-permute-start.26 = (bf16[3,192,544]{2,1,0:T(8,128)(2,1)}, bf16[3,192,544]{2,1,0:T(8,128)(2,1)}, u32[]{:S(2)}, u32[]{:S(2)}) collective-permute-start(bf16[3,192,544]{2,1,0:T(8,128)(2,1)} %broadcast_select_fusion.5), channel_id=1, source_target_pairs={{0,1},{1,0},{2,3},{3,2},{4,5},{5,4},{6,7},{7,6},{8,9},{9,8},{10,11... | collective-permute-start | bytes 1880072 | tf_op jit(solution)/shard_map/ppermute | solution.py:286
  352.6 56.8 %collective-permute-start.36 = (bf16[1088,544]{0,1:T(8,128)(2,1)}, bf16[1088,544]{0,1:T(8,128)(2,1)}, u32[]{:S(2)}, u32[]{:S(2)}) collective-permute-start(bf16[1088,544]{0,1:T(8,128)(2,1)} %broadcast_select_fusion), channel_id=1, source_target_pairs={{0,1},{1,0},{2,3},{3,2},{4,5},{5,4},{6,7},{7,6},{8,9},{9,8},{10,11... | collective-permute-start | bytes 3551240 | tf_op jit(solution)/shard_map/ppermute | solution.py:286
  371.8 20.1 %collective-permute-start.58 = (bf16[544,544]{1,0:T(8,128)(2,1)S(1)}, bf16[544,544]{1,0:T(8,128)(2,1)S(1)}, u32[]{:S(2)}, u32[]{:S(2)}) collective-permute-start(bf16[544,544]{1,0:T(8,128)(2,1)S(1)} %broadcast_select_fusion.9), channel_id=1, source_target_pairs={{0,2},{2,0},{1,3},{3,1},{4,6},{6,4},{5,7},{7,5},{8,10},{10,8},{9,1... | collective-permute-start | bytes 1775624 | tf_op jit(solution)/shard_map/ppermute | solution.py:286
  376.1 30.7 %collective-permute-start.49 = (bf16[544,544]{1,0:T(8,128)(2,1)S(1)}, bf16[544,544]{1,0:T(8,128)(2,1)S(1)}, u32[]{:S(2)}, u32[]{:S(2)}) collective-permute-start(bf16[544,544]{1,0:T(8,128)(2,1)S(1)} %broadcast_select_fusion.10), channel_id=1, source_target_pairs={{0,2},{2,0},{1,3},{3,1},{4,6},{6,4},{5,7},{7,5},{8,10},{10,8},{9,1... | collective-permute-start | bytes 1775624 | tf_op jit(solution)/shard_map/ppermute | solution.py:286
  383.1 34.9 %collective-permute-start.28 = (bf16[3,136,544]{2,1,0:T(8,128)(2,1)}, bf16[3,136,544]{2,1,0:T(8,128)(2,1)}, u32[]{:S(2)}, u32[]{:S(2)}) collective-permute-start(bf16[3,136,544]{2,1,0:T(8,128)(2,1)} %broadcast_select_fusion.23), channel_id=1, source_target_pairs={{0,2},{2,0},{1,3},{3,1},{4,6},{6,4},{5,7},{7,5},{8,10},{10,8},{9,1... | collective-permute-start | bytes 1331720 | tf_op jit(solution)/shard_map/ppermute | solution.py:286
  393.5 27.6 %collective-permute-start.59 = (bf16[136,544]{1,0:T(8,128)(2,1)}, bf16[136,544]{1,0:T(8,128)(2,1)}, u32[]{:S(2)}, u32[]{:S(2)}) collective-permute-start(bf16[136,544]{1,0:T(8,128)(2,1)} %get-tuple-element.107), channel_id=1, source_target_pairs={{0,32},{16,48},{32,0},{48,16},{1,33},{17,49},{33,1},{49,17},{2,34}... | collective-permute-start | bytes 443912 | tf_op jit(solution)/shard_map/ppermute | solution.py:290
  394.7 28.6 %collective-permute-start.61 = (bf16[136,544]{1,0:T(8,128)(2,1)}, bf16[136,544]{1,0:T(8,128)(2,1)}, u32[]{:S(2)}, u32[]{:S(2)}) collective-permute-start(bf16[136,544]{1,0:T(8,128)(2,1)} %get-tuple-element.108), channel_id=1, source_target_pairs={{0,48},{16,0},{32,16},{48,32},{1,49},{17,1},{33,17},{49,33},{2,50}... | collective-permute-start | bytes 443912 | tf_op jit(solution)/shard_map/ppermute | solution.py:290
  406.9 17.4 %collective-permute-start.60 = (bf16[136,544]{1,0:T(8,128)(2,1)}, bf16[136,544]{1,0:T(8,128)(2,1)}, u32[]{:S(2)}, u32[]{:S(2)}) collective-permute-start(bf16[136,544]{1,0:T(8,128)(2,1)} %get-tuple-element.109), channel_id=1, source_target_pairs={{0,16},{16,32},{32,48},{48,0},{1,17},{17,33},{33,49},{49,1},{2,18}... | collective-permute-start | bytes 443912 | tf_op jit(solution)/shard_map/ppermute | solution.py:290
  409.4 22.1 %collective-permute-start.50 = (bf16[136,544]{1,0:T(8,128)(2,1)}, bf16[136,544]{1,0:T(8,128)(2,1)}, u32[]{:S(2)}, u32[]{:S(2)}) collective-permute-start(bf16[136,544]{1,0:T(8,128)(2,1)} %get-tuple-element.114), channel_id=1, source_target_pairs={{0,32},{16,48},{32,0},{48,16},{1,33},{17,49},{33,1},{49,17},{2,34}... | collective-permute-start | bytes 443912 | tf_op jit(solution)/shard_map/ppermute | solution.py:290
  418.0 15.9 %collective-permute-start.52 = (bf16[136,544]{1,0:T(8,128)(2,1)}, bf16[136,544]{1,0:T(8,128)(2,1)}, u32[]{:S(2)}, u32[]{:S(2)}) collective-permute-start(bf16[136,544]{1,0:T(8,128)(2,1)} %get-tuple-element.115), channel_id=1, source_target_pairs={{0,48},{16,0},{32,16},{48,32},{1,49},{17,1},{33,17},{49,33},{2,50}... | collective-permute-start | bytes 443912 | tf_op jit(solution)/shard_map/ppermute | solution.py:290
  428.4 19.8 %collective-permute-start.37 = (bf16[272,544]{1,0:T(8,128)(2,1)S(1)}, bf16[272,544]{1,0:T(8,128)(2,1)S(1)}, u32[]{:S(2)}, u32[]{:S(2)}) collective-permute-start(bf16[272,544]{1,0:T(8,128)(2,1)S(1)} %copy-done.44), channel_id=1, source_target_pairs={{0,8},{4,12},{8,0},{12,4},{1,9},{5,13},{9,1},{13,5},{2,10},{6,14},... | collective-permute-start | bytes 887816 | tf_op jit(solution)/shard_map/ppermute | solution.py:290
  430.5 19.3 %collective-permute-start.39 = (bf16[272,544]{1,0:T(8,128)(2,1)S(1)}, bf16[272,544]{1,0:T(8,128)(2,1)S(1)}, u32[]{:S(2)}, u32[]{:S(2)}) collective-permute-start(bf16[272,544]{1,0:T(8,128)(2,1)S(1)} %copy-done.43), channel_id=1, source_target_pairs={{0,12},{4,0},{8,4},{12,8},{1,13},{5,1},{9,5},{13,9},{2,14},{6,2},{... | collective-permute-start | bytes 887816 | tf_op jit(solution)/shard_map/ppermute | solution.py:290
  431.6 18.7 %collective-permute-start.38 = (bf16[272,544]{1,0:T(8,128)(2,1)S(1)}, bf16[272,544]{1,0:T(8,128)(2,1)S(1)}, u32[]{:S(2)}, u32[]{:S(2)}) collective-permute-start(bf16[272,544]{1,0:T(8,128)(2,1)S(1)} %copy-done.42), channel_id=1, source_target_pairs={{0,4},{4,8},{8,12},{12,0},{1,5},{5,9},{9,13},{13,1},{2,6},{6,10},{... | collective-permute-start | bytes 887816 | tf_op jit(solution)/shard_map/ppermute | solution.py:290
  452.1 10.9 %collective-permute-start.63 = (bf16[136,544]{1,0:T(8,128)(2,1)S(1)}, bf16[136,544]{1,0:T(8,128)(2,1)S(1)}, u32[]{:S(2)}, u32[]{:S(2)}) collective-permute-start(bf16[136,544]{1,0:T(8,128)(2,1)S(1)} %add_convert_fusion.7), channel_id=1, source_target_pairs={{0,48},{16,0},{32,16},{48,32},{1,49},{17,1},{33,17},{49,33},{2,50}... | collective-permute-start | bytes 443912 | tf_op jit(solution)/shard_map/ppermute | solution.py:290
  (107 other events, 917.4 us)

commit v2 on v1

v2 whole, which is shorter than its diff:
```python
import functools

import jax
import jax.numpy as jnp
from jax import lax
from jax.experimental import pallas as pl
from jax.experimental.pallas import tpu as pltpu
from jax.sharding import Mesh
from jax.sharding import PartitionSpec as P


HDIM = 64
D = 1088
HALF = D // 2
TOK = 128
LEN = 1024
SLOT = 192
EPSILON = 1e-05
MASKED = -1e30
DP = ("zl", "y")
ROW = ("x", "zh")
ALL = ("zl", "y", "x", "zh", "c")
MESH = pl.DeviceIdType.MESH
PART = 68
BF = jnp.bfloat16
F32 = jnp.float32


class Links:
    def __init__(self, send, recv, local):
        self.send, self.recv, self.local = send, recv, local
        self.pushed, self.kept = [], []
        self.x, self.c, self.y = lax.axis_index("x"), lax.axis_index("c"), lax.axis_index("y")
        self.zh, self.zl = lax.axis_index("zh"), lax.axis_index("zl")
        self.rank = 2 * self.x + self.c
        self.sibling = {"c": 1 - self.c}
        self.partner = {"zh": 1 - self.zh}

    def along_x(self, k):
        return {"x": lax.rem(self.x + k, 4)}

    def along_y(self, k):
        return {"y": lax.rem(self.y + k, 4)}

    def line(self):
        found = []
        for k, j in ((2, 0), (2, 1), (1, 0), (1, 1), (3, 0), (3, 1), (0, 1)):
            found.append((lax.rem(self.x + k, 4), lax.rem(self.c + j, 2)))
        return [({"x": x, "c": c}, 2 * x + c) for x, c in found]

    def plane(self, both=True):
        found = []
        for h in (1, 0) if both else (0,):
            for l in (1, 0):
                for k in (2, 1, 3, 0):
                    if h or l or k:
                        y, zl = lax.rem(self.y + k, 4), lax.rem(self.zl + l, 2)
                        zh = lax.rem(self.zh + h, 2)
                        found.append(({"y": y, "zl": zl, "zh": zh}, zh, 2 * y + zl))
        return found

    def greet(self, targets):
        barrier = pltpu.get_barrier_semaphore()
        for target in targets:
            pl.semaphore_signal(barrier, inc=1, device_id=target, device_id_type=MESH)
        pl.semaphore_wait(barrier, len(targets))

    def push(self, src, dst, target):
        n = len(self.pushed)
        copy = pltpu.make_async_remote_copy(
            src_ref=src,
            dst_ref=dst,
            send_sem=self.send.at[n],
            recv_sem=self.recv.at[n],
            device_id=target,
            device_id_type=MESH,
        )
        copy.start()
        self.pushed.append([copy, False])
        return n

    def arrived(self, n):
        if not self.pushed[n][1]:
            self.pushed[n][0].wait_recv()
            self.pushed[n][1] = True

    def keep(self, src, dst):
        n = len(self.kept)
        copy = pltpu.make_async_copy(src, dst, self.local.at[n])
        copy.start()
        self.kept.append([copy, False])
        return n

    def stored(self, n):
        if not self.kept[n][1]:
            self.kept[n][0].wait()
            self.kept[n][1] = True

    def finish(self):
        for n in range(len(self.kept)):
            self.stored(n)
        for n in range(len(self.pushed)):
            self.arrived(n)
        for copy, _ in self.pushed:
            copy.wait_send()


SEMS = [pltpu.SemaphoreType.DMA((64,)), pltpu.SemaphoreType.DMA((64,)), pltpu.SemaphoreType.DMA((32,))]
SPACES = {"v": pltpu.VMEM, "h": pl.ANY}


def call(kernel, name, cid, args, spaces, outs, scratch=()):
    return pl.pallas_call(
        kernel,
        out_shape=tuple(jax.ShapeDtypeStruct(shape, dtype) for _, shape, dtype in outs),
        in_specs=[pl.BlockSpec(memory_space=SPACES[s]) for s in spaces],
        out_specs=tuple(pl.BlockSpec(memory_space=SPACES[s]) for s, _, _ in outs),
        scratch_shapes=[*scratch, *SEMS],
        compiler_params=pltpu.CompilerParams(
            collective_id=cid, has_side_effects=True, vmem_limit_bytes=44 << 20
        ),
        name=name,
    )(*args)


class Gather:
    def __init__(self, links, a_ref, o_ref):
        self.links, self.o = links, o_ref
        links.keep(a_ref, o_ref.at[links.rank])
        self.far = {k: links.push(a_ref, o_ref.at[links.rank], links.along_x(k)) for k in (2, 1, 3)}
        links.push(a_ref, o_ref.at[links.rank], links.sibling)

    def forward(self, k):
        links = self.links
        links.arrived(self.far[k])
        slot = 2 * lax.rem(links.x + 4 - k, 4) + links.c
        links.push(self.o.at[slot], self.o.at[slot], links.sibling)


class Scatter:
    def __init__(self, links, p_ref, near, out, came):
        self.links, self.p, self.near, self.out, self.came = links, p_ref, near, out, came
        self.swaps = {}
        for k in (2, 1, 3, 0):
            to = lax.rem(links.x + k, 4)
            self.swaps[k] = links.push(p_ref.at[2 * to + 1 - links.c], near.at[k], links.sibling)
        self.sends = {}

    def both(self, k):
        links = self.links
        links.arrived(self.swaps[k])
        to = lax.rem(links.x + k, 4)
        return self.p[2 * to + links.c].astype(F32) + self.near[k].astype(F32)

    def forward(self):
        for k in (2, 1, 3):
            self.out[k] = self.both(k).astype(BF)
            self.sends[k] = self.links.push(self.out.at[k], self.came.at[k], self.links.along_x(k))

    def total(self):
        total = self.both(0)
        for k in (1, 3, 2):
            self.links.arrived(self.sends[k])
            total += self.came[k].astype(F32)
        return total


SCATTER_ROOM = [pltpu.VMEM((4, TOK, D), BF)] * 3
PIECES = (8, PART, HALF)
GRADS_ROOM = [pltpu.VMEM((2, *PIECES), BF), pltpu.VMEM((16, PART, HALF), BF)]


class GradScatter:
    def __init__(self, links, parts, came):
        self.links, self.parts, self.came = links, parts, came

    @staticmethod
    def between_cores(links, own, parts):
        kept = links.keep(own.at[links.c], parts.at[links.c])
        swap = links.push(own.at[1 - links.c], parts.at[links.c], links.sibling)
        return kept, swap

    def start(self):
        self.sends = [
            self.links.push(self.parts.at[zh, piece], self.came.at[n + 1], target)
            for n, (target, zh, piece) in enumerate(self.links.plane())
        ]

    def total(self):
        links = self.links
        total = self.parts[links.zh, 2 * links.y + links.zl].astype(F32)
        for n, send in enumerate(self.sends):
            links.arrived(send)
            total += self.came[n + 1].astype(F32)
        return total.astype(BF)


def spread_grads(links, piece_ref, o_ref):
    slot = o_ref.at[2 * links.y + links.zl]
    links.keep(piece_ref, slot)
    for target, _, _ in links.plane(both=False):
        links.push(piece_ref, slot, target)


def targets(links, *groups):
    found = []
    for group in groups:
        if group == "x":
            found += [links.along_x(k) for k in (1, 2, 3)]
        if group == "y":
            found += [links.along_y(k) for k in (1, 2, 3)]
        if group == "c":
            found.append(links.sibling)
        if group == "z":
            found.append(links.partner)
        if group == "line":
            found += [target for target, _ in links.line()]
        if group == "plane":
            found += [target for target, _, _ in links.plane()]
    return found


def enter_kernel(a_ref, wo_ref, cols_ref, tok_ref, wo4_ref, colso_ref, pair, *sems):
    links = Links(*sems)
    x, zh, c = links.x, links.zh, links.c
    links.greet(targets(links, "x", "c", "z"))
    other = links.push(a_ref.at[1 - zh], pair.at[zh], links.partner)
    mine = links.keep(a_ref.at[zh], pair.at[zh])
    for k in (2, 1, 3):
        links.push(wo_ref, wo4_ref.at[x], links.along_x(k))
    links.keep(wo_ref, wo4_ref.at[x])
    links.push(cols_ref, colso_ref.at[c], links.sibling)
    links.keep(cols_ref, colso_ref.at[c])
    links.stored(mine)
    links.arrived(other)
    links.push(pair.at[1 - c], tok_ref.at[c], links.sibling)
    links.keep(pair.at[c], tok_ref.at[c])
    links.finish()


def enter(block_in, output_weight, columns):
    return call(
        enter_kernel,
        "enter",
        1,
        (block_in, output_weight, columns),
        "hhv",
        [("v", (2, TOK, HALF), BF), ("h", (4, 136, HALF), BF), ("v", (2, 8, HALF), F32)],
        [pltpu.VMEM((2, TOK, HALF), BF)],
    )


def first_kernel(n_ref, t_ref, w_ref, tail_ref, rows_ref, wo4_ref, o_ref, to_ref, wq_ref, tails_ref, rowso_ref, woo_ref, pair, mid, *sems):
    links = Links(*sems)
    x, y, zh, c = links.x, links.y, links.zh, links.c
    right, left = lax.rem(x + 1, 4), lax.rem(x + 3, 4)
    diagonal = [{"x": right, "zh": 1 - zh}, {"x": left, "zh": 1 - zh}]
    links.greet(targets(links, "x", "y", "c", "z") + diagonal)
    gather = Gather(links, n_ref, o_ref)
    t_other = links.push(t_ref.at[1 - zh], pair.at[zh], links.partner)
    t_mine = links.keep(t_ref.at[zh], pair.at[zh])
    wo_own = links.push(wo4_ref.at[y], mid, links.partner)
    rows_other = links.push(rows_ref, rowso_ref.at[zh], links.partner)
    links.keep(rows_ref, rowso_ref.at[zh])
    w_other = links.push(w_ref, wq_ref.at[c, zh], links.partner)
    links.keep(w_ref, wq_ref.at[c, zh])
    links.push(w_ref, wq_ref.at[c, zh], links.sibling)
    n = len(links.pushed)
    shifts = []
    for i, target in enumerate(({"x": right}, diagonal[0])):
        for j, (src, dst) in enumerate(((tail_ref, tails_ref.at[c]), (rows_ref, rowso_ref.at[2]))):
            shifts.append(
                pltpu.make_async_remote_copy(
                    src_ref=src,
                    dst_ref=dst,
                    send_sem=links.send.at[50 + 2 * i + j],
                    recv_sem=links.recv.at[50 + j],
                    device_id=target,
                    device_id_type=MESH,
                )
            )

    @pl.when(zh == 1)
    def _():
        for copy in shifts:
            copy.start()

    links.keep(wo4_ref, woo_ref.at[c, zh])
    links.push(wo4_ref, woo_ref.at[c, zh], links.sibling)
    gather.forward(1)
    gather.forward(3)
    links.stored(t_mine)
    links.arrived(t_other)
    links.push(pair.at[1 - c], to_ref.at[c], links.sibling)
    links.keep(pair.at[c], to_ref.at[c])
    links.arrived(wo_own)
    slot = woo_ref.at[c, 1 - zh, y]
    links.keep(mid, slot)
    round_y = [links.push(mid, slot, links.along_y(k)) for k in (2, 1, 3)]
    links.push(mid, slot, links.sibling)
    shifts[0].wait_recv()
    shifts[1].wait_recv()
    links.push(tails_ref.at[c], tails_ref.at[c], links.sibling)
    for k, copy in zip((2, 1, 3), round_y):
        links.arrived(copy)
        slot = woo_ref.at[c, 1 - zh, lax.rem(y + 4 - k, 4)]
        links.push(slot, slot, links.sibling)
    links.arrived(w_other)
    slot = wq_ref.at[c, 1 - zh]
    links.push(slot, slot, links.sibling)
    gather.forward(2)
    links.finish()

    @pl.when(zh == 1)
    def _():
        for copy in shifts:
            copy.wait_send()


def first(normed, out_grad, w, tail, rows, wo4):
    return call(
        first_kernel,
        "first",
        2,
        (normed, out_grad, w, tail, rows, wo4),
        "vhhhvh",
        [
            ("v", (8, TOK, D), BF),
            ("v", (2, TOK, HALF), BF),
            ("h", (2, 2, 3, 136, HALF), BF),
            ("h", (2, 3, 48, HALF), BF),
            ("v", (3, 8, 128), F32),
            ("h", (2, 2, 4, 136, HALF), BF),
        ],
        [pltpu.VMEM((2, TOK, HALF), BF), pltpu.VMEM((136, HALF), BF)],
    )


BLOCK = 256


def dot(a, b, dims):
    return lax.dot_general(a, b, (dims, ((), ())), preferred_element_type=F32)


def attend_head(qkv_ref, h, m_ref, p_ref):
    keys = lax.broadcasted_iota(jnp.int32, (BLOCK, BLOCK), 0)
    queries = lax.broadcasted_iota(jnp.int32, (BLOCK, BLOCK), 1)
    head = pl.ds(h * HDIM, HDIM)
    for i in range(LEN // BLOCK):
        low, high = i * BLOCK, (i + 1) * BLOCK
        q = qkv_ref[0, head, low:high] * BF(HDIM**-0.5)
        parts = [dot(qkv_ref[1, head, low:high], q, ((0,), (0,)))]
        parts[0] = jnp.where(keys <= queries, parts[0], MASKED)
        if i:
            parts.insert(0, dot(qkv_ref[1, head, :low], q, ((0,), (0,))))
        highest = functools.reduce(jnp.maximum, [jnp.max(s, axis=0, keepdims=True) for s in parts])
        parts = [jnp.exp(s - highest) for s in parts]
        share = 1.0 / sum(jnp.sum(s, axis=0, keepdims=True) for s in parts)
        parts = [(s * share).astype(BF) for s in parts]
        p_ref[h, low:high, low:high] = parts[-1]
        mixed = dot(qkv_ref[2, head, low:high], parts[-1], ((1,), (0,)))
        if i:
            p_ref[h, :low, low:high] = parts[0]
            mixed += dot(qkv_ref[2, head, :low], parts[0], ((1,), (0,)))
        m_ref[head, low:high] = mixed.astype(BF)


def attend_kernel(qkv_ref, t_ref, m_ref, p_ref, f_ref, o_ref, *sems):
    links = Links(*sems)
    links.greet(targets(links, "line"))
    gather = Gather(links, t_ref, o_ref)
    for h in range(SLOT // HDIM):
        attend_head(qkv_ref, h, m_ref, p_ref)
    own = links.rank
    columns = pl.ds(pl.multiple_of(own * TOK, TOK), TOK)
    links.keep(m_ref.at[:, columns], f_ref.at[own])
    for target, rank in links.line():
        columns = pl.ds(pl.multiple_of(rank * TOK, TOK), TOK)
        links.push(m_ref.at[:, columns], f_ref.at[own], target)
    for k in (1, 3, 2):
        gather.forward(k)
    links.finish()


def attend(qkv, tangent):
    return call(
        attend_kernel,
        "attend",
        3,
        (qkv, tangent),
        "vv",
        [
            ("v", (SLOT, LEN), BF),
            ("v", (SLOT // HDIM, LEN, LEN), BF),
            ("v", (8, SLOT, TOK), BF),
            ("v", (8, TOK, D), BF),
        ],
    )


def second_kernel(n_ref, up_ref, down_ref, o_ref, upo_ref, downo_ref, up_pair, down_pair, *sems):
    links = Links(*sems)
    y, zh, c = links.y, links.zh, links.c
    links.greet(targets(links, "x", "y", "c", "z"))
    gather = Gather(links, n_ref, o_ref)
    crossed = []
    for w_ref, pair in ((up_ref, up_pair), (down_ref, down_pair)):
        crossed.append((links.push(w_ref.at[y], pair.at[zh, y], links.partner), links.keep(w_ref, pair.at[zh])))
    turned = []
    for (other, _), pair in zip(crossed, (up_pair, down_pair)):
        links.arrived(other)
        slot = pair.at[1 - zh, y]
        turned.append([links.push(slot, slot, links.along_y(k)) for k in (2, 1, 3)])
    gather.forward(1)
    gather.forward(3)
    for (_, kept), copies, pair, out in zip(crossed, turned, (up_pair, down_pair), (upo_ref, downo_ref)):
        links.stored(kept)
        for copy in copies:
            links.arrived(copy)
        links.push(pair.at[1 - c], out.at[c], links.sibling)
        links.keep(pair.at[c], out.at[c])
    gather.forward(2)
    links.finish()


def second(normed, up, down):
    return call(
        second_kernel,
        "second",
        4,
        (normed, up, down),
        "vhh",
        [("v", (8, TOK, D), BF), ("v", (2, 4, 136, HALF), BF), ("v", (2, 4, 136, HALF), BF)],
        [pltpu.VMEM((2, 4, 136, HALF), BF)] * 2,
    )


def hidden_kernel(n_ref, t_ref, up_ref, down_ref, b_ref, low_ref, dn_ref, gup_ref, gdown_ref, gb_ref, up, down, up_sum, down_sum):
    step = pl.program_id(0)

    @pl.when(step == 0)
    def _():
        for h in range(2):
            up[:, h * HALF : (h + 1) * HALF] = up_ref[h]
            down[:, h * HALF : (h + 1) * HALF] = down_ref[h]
        up_sum[...] = jnp.zeros_like(up_sum)
        down_sum[...] = jnp.zeros_like(down_sum)
        gb_ref[...] = jnp.zeros_like(gb_ref)

    n = n_ref[...].reshape(BLOCK, D)
    t = t_ref[...].reshape(BLOCK, D)
    pre = dot(n, up[...], ((1,), (1,))) + b_ref[...]
    cumulative = 0.5 * (1.0 + lax.erf(pre * 0.7071067811865476))
    density = jnp.exp(-0.5 * pre * pre) * 0.3989422804014327
    active = (pre * cumulative).astype(BF)
    slope = cumulative + pre * density
    low_ref[...] = dot(active, down[...], ((1,), (0,))).astype(BF).reshape(low_ref.shape)
    d_pre = (dot(t, down[...], ((1,), (1,))) * slope).astype(BF)
    dn_ref[...] = dot(d_pre, up[...], ((1,), (0,))).astype(BF).reshape(dn_ref.shape)
    down_sum[...] += dot(active, t, ((0,), (0,)))
    up_sum[...] += dot(d_pre, n, ((0,), (0,)))
    gb_ref[...] += jnp.sum(d_pre.astype(F32), axis=0, keepdims=True)

    @pl.when(step == pl.num_programs(0) - 1)
    def _():
        for h in range(2):
            for out, total in ((gup_ref, up_sum), (gdown_ref, down_sum)):
                for j in range(8):
                    out[h, j] = total[j * PART : (j + 1) * PART, h * HALF : (h + 1) * HALF].astype(BF)


def hidden_part(second_rows, tangent_rows, up, down, bias):
    rows = pl.BlockSpec((BLOCK // TOK, TOK, D), lambda i: (i, 0, 0))
    weight = pl.BlockSpec((2, HALF, HALF), lambda i: (0, 0, 0))
    grad = pl.BlockSpec((2, *PIECES), lambda i: (0, 0, 0, 0))
    one = pl.BlockSpec((1, HALF), lambda i: (0, 0))
    return pl.pallas_call(
        hidden_kernel,
        grid=(LEN // BLOCK,),
        in_specs=[rows, rows, weight, weight, one],
        out_specs=(rows, rows, grad, grad, one),
        out_shape=(
            jax.ShapeDtypeStruct((8, TOK, D), BF),
            jax.ShapeDtypeStruct((8, TOK, D), BF),
            jax.ShapeDtypeStruct((2, *PIECES), BF),
            jax.ShapeDtypeStruct((2, *PIECES), BF),
            jax.ShapeDtypeStruct((1, HALF), F32),
        ),
        scratch_shapes=[pltpu.VMEM((HALF, D), BF)] * 2 + [pltpu.VMEM((HALF, D), F32)] * 2,
        compiler_params=pltpu.CompilerParams(vmem_limit_bytes=44 << 20),
        name="hidden_part",
    )(second_rows, tangent_rows, up, down, bias)


def third_kernel(p_ref, g_ref, o_ref, piece_ref, near, out, came, parts, found, *sems):
    links = Links(*sems)
    links.greet(targets(links, "x", "c", "plane"))
    scatter = Scatter(links, p_ref, near, out, came)
    grads = GradScatter(links, parts, found)
    kept, swap = grads.between_cores(links, g_ref, parts)
    scatter.forward()
    links.stored(kept)
    links.arrived(swap)
    grads.start()
    o_ref[...] = scatter.total()
    piece_ref[...] = grads.total()
    links.finish()


def third(d_normed, grad):
    return call(
        third_kernel,
        "third",
        5,
        (d_normed, grad),
        "vv",
        [("v", (TOK, D), F32), ("v", (PART, HALF), BF)],
        SCATTER_ROOM + GRADS_ROOM,
    )


def attend_back_head(qkv_ref, h, u_ref, p_ref, d_ref, dk_sum, dv_sum):
    head = pl.ds(h * HDIM, HDIM)
    for i in range(LEN // BLOCK):
        low, high = i * BLOCK, (i + 1) * BLOCK
        q = qkv_ref[0, head, low:high] * BF(HDIM**-0.5)
        u = u_ref[head, low:high]
        p = p_ref[h, :high, low:high]
        wide = p.astype(F32)
        dp = dot(qkv_ref[2, head, :high], u, ((0,), (0,)))
        centre = jnp.sum(wide * dp, axis=0, keepdims=True)
        ds = (wide * (dp - centre)).astype(BF)
        d_ref[0, head, low:high] = (dot(qkv_ref[1, head, :high], ds, ((1,), (0,))) * HDIM**-0.5).astype(BF)
        dk = dot(q, ds, ((1,), (1,)))
        dv = dot(u, p, ((1,), (1,)))
        if i:
            dk_sum[:, :low] += dk[:, :low]
            dv_sum[:, :low] += dv[:, :low]
        dk_sum[:, low:high] = dk[:, low:]
        dv_sum[:, low:high] = dv[:, low:]
    d_ref[1, head] = dk_sum[...].astype(BF)
    d_ref[2, head] = dv_sum[...].astype(BF)


def back_kernel(m_ref, a_ref, qkv_ref, p_ref, g_ref, d_ref, o_ref, piece_ref, u, dk_sum, dv_sum, parts, found, *sems):
    links = Links(*sems)
    links.greet(targets(links, "line", "plane"))
    own = links.rank
    columns = pl.ds(pl.multiple_of(own * TOK, TOK), TOK)

    def rows(rank):
        return pl.ds(pl.multiple_of(rank * 2 * HDIM, 2 * HDIM), SLOT)

    mine = links.keep(m_ref.at[rows(own)], u.at[:, columns])
    others = [links.push(m_ref.at[rows(rank)], u.at[:, columns], target) for target, rank in links.line()]
    gather = Gather(links, a_ref, o_ref)
    grads = GradScatter(links, parts, found)
    kept, swap = grads.between_cores(links, g_ref, parts)
    links.stored(kept)
    links.arrived(swap)
    grads.start()
    links.stored(mine)
    for copy in others:
        links.arrived(copy)
    for h in range(SLOT // HDIM):
        attend_back_head(qkv_ref, h, u, p_ref, d_ref, dk_sum, dv_sum)
    for k in (1, 3, 2):
        gather.forward(k)
    piece_ref[...] = grads.total()
    links.finish()


def back(d_mixed, d_attended, qkv, probs, grad):
    return call(
        back_kernel,
        "back",
        6,
        (d_mixed, d_attended, qkv, probs, grad),
        "vvvvv",
        [("v", (3, SLOT, LEN), BF), ("v", (8, TOK, D), BF), ("v", (PART, HALF), BF)],
        [pltpu.VMEM((SLOT, LEN), BF)] + [pltpu.VMEM((HDIM, LEN), F32)] * 2 + GRADS_ROOM,
    )


def fourth_kernel(p_ref, up_ref, down_ref, s_ref, o_ref, gup_ref, gdown_ref, chip_ref, tail_ref, near, out, came, *sems):
    links = Links(*sems)
    c = links.c
    links.greet(targets(links, "x", "c", "plane"))
    scatter = Scatter(links, p_ref, near, out, came)
    kept = links.keep(s_ref.at[c], chip_ref.at[c])
    swap = links.push(s_ref.at[1 - c], chip_ref.at[c], links.sibling)
    spread_grads(links, up_ref, gup_ref)
    spread_grads(links, down_ref, gdown_ref)
    scatter.forward()
    links.stored(kept)
    links.arrived(swap)
    links.push(chip_ref.at[0, :, pl.ds(0, 48)], tail_ref, links.along_x(3))
    o_ref[...] = scatter.total()
    links.finish()


def fourth(d_normed, up_piece, down_piece, slots):
    return call(
        fourth_kernel,
        "fourth",
        7,
        (d_normed, up_piece, down_piece, slots),
        "vvvv",
        [
            ("v", (TOK, D), F32),
            ("h", PIECES, BF),
            ("h", PIECES, BF),
            ("v", (2, 4, SLOT, HALF), BF),
            ("v", (4, 48, HALF), BF),
        ],
        SCATTER_ROOM,
    )


def leave_kernel(p_ref, r_ref, i_ref, g_ref, v_ref, b_ref, oo_ref, io_ref, go_ref, vo_ref, near, out, came, found, piece, halves_o, pair_o, pair_i, v_line, v_own, v_plane, v_sum, *sems):
    links = Links(*sems)
    y, zh, zl, c = links.y, links.zh, links.zl, links.c
    links.greet(targets(links, "line", "plane"))
    scatter = Scatter(links, p_ref, near, out, came)
    grads = GradScatter(links, g_ref, found)
    line = [links.push(v_ref.at[rank], v_line.at[n], target) for n, (target, rank) in enumerate(links.line())]

    def between_cores(src, pair):
        return links.keep(src.at[c], pair.at[c]), links.push(src.at[1 - c], pair.at[c], links.sibling)

    def to_partner(src, pair, dst, copies):
        links.stored(copies[0])
        links.arrived(copies[1])
        links.push(pair.at[1 - zh], dst.at[zh], links.partner)
        links.keep(pair.at[zh], dst.at[zh])

    copies = between_cores(i_ref, pair_i)
    scatter.forward()
    grads.start()
    to_partner(i_ref, pair_i, io_ref, copies)
    total = v_ref[links.rank]
    for n, copy in enumerate(line):
        links.arrived(copy)
        total += v_line[n]
    v_own[pl.ds(0, 16)] = total
    v_own[pl.ds(16, 8)] = b_ref[...]
    place = (2 * zh + zl) * 4 + y
    kept = links.keep(v_own, v_plane.at[place])
    plane = [links.push(v_own, v_plane.at[place], target) for target, _, _ in links.plane()]
    links.stored(kept)
    for copy in plane:
        links.arrived(copy)
    total = v_plane[0]
    for n in range(1, 16):
        total += v_plane[n]
    v_sum[...] = total
    links.keep(v_sum, vo_ref.at[links.rank])
    for target, _ in links.line():
        links.push(v_sum, vo_ref.at[links.rank], target)
    result = (scatter.total() + r_ref[...]).astype(BF)
    halves_o[0] = result[:, :HALF]
    halves_o[1] = result[:, HALF:]
    copies = between_cores(halves_o, pair_o)
    piece[...] = grads.total()
    spread_grads(links, piece, go_ref)
    to_partner(halves_o, pair_o, oo_ref, copies)
    links.finish()


def leave(lowered, residual, in_grad, grads, vectors, bias_up):
    pair = pltpu.VMEM((2, TOK, HALF), BF)
    return call(
        leave_kernel,
        "leave",
        8,
        (lowered, residual, in_grad, grads, vectors, bias_up),
        "vvvvvv",
        [
            ("v", (2, TOK, HALF), BF),
            ("v", (2, TOK, HALF), BF),
            ("v", PIECES, BF),
            ("v", (8, 24, 128), F32),
        ],
        SCATTER_ROOM
        + [GRADS_ROOM[1], pltpu.VMEM((PART, HALF), BF), pair, pair, pair]
        + [pltpu.VMEM((7, 16, 128), F32), pltpu.VMEM((24, 128), F32)]
        + [pltpu.VMEM((16, 24, 128), F32), pltpu.VMEM((24, 128), F32)],
    )


def normed(values, gain, shift):
    centre = jnp.mean(values, axis=1, keepdims=True)
    second_moment = jnp.mean(values * values, axis=1, keepdims=True)
    inverse = lax.rsqrt(second_moment - centre * centre + EPSILON)
    centred = (values - centre) * inverse
    return (centred * gain + shift).astype(BF), centred, inverse


def normed_back(upstream, centred, inverse, gain):
    scaled = upstream * gain
    result = inverse * (
        scaled
        - jnp.mean(scaled, axis=1, keepdims=True)
        - centred * jnp.mean(scaled * centred, axis=1, keepdims=True)
    )
    return result, jnp.sum(upstream * centred, axis=0), jnp.sum(upstream, axis=0)


def joined(halves):
    return jnp.concatenate([halves[0], halves[1]], axis=-1)


def parted(whole):
    return jnp.stack([whole[..., :HALF], whole[..., HALF:]])


def per_device(
    block_in,
    query_key_value_weight,
    bias_qv,
    output_weight,
    bias_out,
    gain_one,
    shift_one,
    gain_two,
    shift_two,
    up_weight,
    bias_up,
    down_weight,
    bias_down,
    out_grad,
):
    x, zh, c = (lax.axis_index(a) for a in ("x", "zh", "c"))
    rank = 2 * x + c
    last = rank == 7
    real = jnp.logical_or(jnp.arange(SLOT) < 128, last)

    columns = jnp.stack([bias_out, gain_one, shift_one, gain_two, shift_two, bias_down, bias_down, bias_down])
    tokens, wo4, columns = enter(block_in, output_weight, columns)
    inputs = joined(tokens).astype(F32)
    bias_out, gain_one, shift_one, gain_two, shift_two, bias_down = joined(columns)[:6]
    normed_one, centred_one, inverse_one = normed(inputs, gain_one, shift_one)
    rows = jnp.concatenate([bias_qv.reshape(-1), bias_up, jnp.zeros((208,), F32)]).reshape(8, 128)
    first_rows, tangent, wq, tails, rows, wo = first(
        normed_one, out_grad, query_key_value_weight, query_key_value_weight[:, 88:], rows, wo4
    )
    tangent = joined(tangent)

    def slots(before, chip):
        width = chip.ndim - 2
        spare = jnp.zeros((*chip.shape[:-2], 48, chip.shape[-1]), chip.dtype)
        chip = jnp.concatenate([before, chip, spare], axis=width)
        return lax.dynamic_slice_in_dim(chip, 48 - 16 * x + 128 * c, SLOT, width)

    w = [
        slots(tails[h], jnp.concatenate([wq[h, 0], wq[h, 1]], axis=1)) for h in range(2)
    ]
    weight_qkv = jnp.where(real[None, :, None], joined(w), BF(0))
    rows = rows.reshape(3, 1024)
    bias_up = lax.dynamic_slice(rows, (c, 272), (1, HALF))
    qv = rows[:, :272].reshape(3, 2, 136)
    qv = slots(qv[2, :, 88:, None], jnp.concatenate([qv[0], qv[1]], axis=1)[..., None])[..., 0]
    qv = jnp.where(real[None], qv, 0.0)
    bias_qkv = jnp.stack([qv[0], jnp.zeros_like(qv[0]), qv[1]])

    flat_rows = first_rows.reshape(LEN, D)
    qkv = jnp.einsum("koi,ti->kot", weight_qkv, flat_rows, preferred_element_type=F32)
    qkv = (qkv + bias_qkv[..., None]).astype(BF)
    mixed, probs, found, tangent_rows = attend(qkv, tangent)
    mixed_here = jnp.concatenate([found[:7, :128].reshape(896, TOK), found[7]])
    wo = jnp.transpose(wo, (0, 2, 1, 3, 4)).reshape(2, D, HALF)
    attended = [jnp.einsum("ft,fo->to", mixed_here, wo[h], preferred_element_type=F32) for h in range(2)]
    residual = inputs + (joined(attended) + bias_out)

    normed_two, centred_two, inverse_two = normed(residual, gain_two, shift_two)
    quarters = (4, 136, HALF)
    second_rows, up, down = second(normed_two, up_weight.reshape(quarters), down_weight.reshape(quarters))
    lowered, d_normed_two, up_grad, down_grad, grad_bias_up = hidden_part(
        second_rows,
        tangent_rows,
        up.reshape(2, HALF, HALF),
        down.reshape(2, HALF, HALF),
        bias_up,
    )
    d_normed_two, down_piece = third(d_normed_two, down_grad)
    tangent = tangent.astype(F32)
    grad_bias_down = jnp.sum(tangent, axis=0)
    part, grad_gain_two, grad_shift_two = normed_back(d_normed_two, centred_two, inverse_two, gain_two)
    d_residual = tangent + part
    d_attended = d_residual.astype(BF)
    grad_bias_out = jnp.sum(d_attended, axis=0, dtype=F32)

    d_mixed = sum(
        jnp.einsum("fo,to->ft", wo[h], d_attended[:, h * HALF : (h + 1) * HALF], preferred_element_type=F32)
        for h in range(2)
    ).astype(BF)
    d_qkv, attended_rows, up_piece = back(d_mixed, d_attended, qkv, probs, up_grad)
    attended_rows = attended_rows.reshape(LEN, D)
    d_normed_one = jnp.einsum("kot,koi->ti", d_qkv, weight_qkv, preferred_element_type=F32).astype(BF)
    grad_qkv = jnp.einsum("kot,ti->koi", d_qkv, flat_rows, preferred_element_type=F32).astype(BF)
    grad_out = jnp.einsum("ft,to->fo", mixed, attended_rows, preferred_element_type=F32).astype(BF)
    grads = parted(jnp.concatenate([grad_qkv, grad_out[None]]))
    d_normed_one, up_grad, down_grad, chip, tail = fourth(
        d_normed_one.reshape(8, TOK, D), up_piece, down_piece, grads
    )
    tail = jnp.pad(tail, ((0, 0), (0, 16), (0, 0)))
    chip = jnp.concatenate([chip[0, :, :128], chip[1, :, :128], jnp.where(x == 3, chip[1, :, 128:], tail)], axis=1)
    chip = lax.dynamic_slice_in_dim(chip, 16 * x, 272, 1)
    chip = jnp.transpose(chip.reshape(4, 2, 2, PART, HALF), (1, 0, 2, 3, 4)).reshape(2, *PIECES)

    part, grad_gain_one, grad_shift_one = normed_back(d_normed_one, centred_one, inverse_one, gain_one)
    in_grad = parted((d_residual + part).astype(BF))

    bias_sums = jnp.sum(d_qkv, axis=2, dtype=F32)
    bias_sums = jnp.where(real[None], jnp.stack([bias_sums[0], bias_sums[2]]), 0.0)
    wide = lax.dynamic_update_slice(jnp.zeros((2, D), F32), bias_sums, (0, 128 * rank))
    vectors = jnp.stack(
        [grad_bias_out, grad_gain_one, grad_shift_one, grad_gain_two, grad_shift_two, grad_bias_down, wide[0], wide[1]]
    )
    vectors = jnp.pad(vectors, ((0, 0), (0, 2048 - D))).reshape(8, 16, 128)
    grad_bias_up = jnp.pad(grad_bias_up.reshape(-1), (0, 480)).reshape(8, 128)
    block_out, in_grad, grads, vectors = leave(lowered, residual + bias_down, in_grad, chip, vectors, grad_bias_up)
    grads = grads.reshape(4, 136, HALF).astype(F32)
    row = 2 * x + zh
    grad_bias_up = lax.dynamic_index_in_dim(vectors, row, 0, keepdims=False)[16:].reshape(-1)[:HALF]
    vectors = vectors[:, :16].reshape(8, 2048)[:, :D]
    six = lax.dynamic_slice_in_dim(vectors[:6], HALF * c, HALF, 1)
    grad_bias_out, grad_gain_one, grad_shift_one, grad_gain_two, grad_shift_two, grad_bias_down = six
    grad_bias_qv = lax.dynamic_slice_in_dim(vectors[6:], 136 * row, 136, 1)

    return (
        block_out,
        in_grad.astype(F32),
        grads[:3],
        grad_bias_qv,
        grads[3],
        grad_bias_out,
        grad_gain_one,
        grad_shift_one,
        grad_gain_two,
        grad_shift_two,
        up_grad.reshape(HALF, HALF).astype(F32),
        grad_bias_up,
        down_grad.reshape(HALF, HALF).astype(F32),
        grad_bias_down,
    )


def solution(mesh):
    finer = Mesh(mesh.devices.reshape(2, 4, 4, 2, 2), ALL)
    return jax.shard_map(
        per_device,
        mesh=finer,
        in_specs=(
            P(DP, ROW, "c"),
            P(None, ROW, "c"),
            P(None, ROW),
            P(ROW, "c"),
            P("c"),
            P("c"),
            P("c"),
            P("c"),
            P("c"),
            P(ROW, "c"),
            P(ROW),
            P(ROW, "c"),
            P("c"),
            P(DP, ROW, "c"),
        ),
        out_specs=(
            P(DP, ROW, "c"),
            P(DP, ROW, "c"),
            P(None, ROW, "c"),
            P(None, ROW),
            P(ROW, "c"),
            P("c"),
            P("c"),
            P("c"),
            P("c"),
            P("c"),
            P(ROW, "c"),
            P(ROW),
            P(ROW, "c"),
            P("c"),
        ),
        check_vma=False,
    )
```

time: 498 us -> 345 us (0.69)
  Pallas kernels: 143 us -> 263 us
  starting transfers between devices: 77.4 us -> 0 us
  waiting for transfers between devices: 74.8 us -> 0 us
  blocking collectives: 67.1 us -> 0 us
  other arithmetic: 46 us -> 13.5 us
  matrix products: 31 us -> 13.6 us
    pallas_call x10 -> x9, Pallas kernels: 143 us -> 263 us  [the longest x8 246 us: call(): pl.pallas_call(kernel, out_shape=tuple((jax.ShapeDtypeStruct(shape, dtype...]
    ppermute x66 -> x0, starting transfers between devices: 77.4 us -> none  [the longest x36 46.9 us: shifted(): return lax.ppermute(a, axis, [(i, (i + k) % 4) for i in range(4)])]
    ppermute x66 -> x0, waiting for transfers between devices: 74.8 us -> none  [the longest x30 52.5 us: swap(): return lax.ppermute(a, axis, [(0, 1), (1, 0)])]
    psum x1 -> x0, blocking collectives: 67.1 us -> none  [per_device(): vector = lax.psum(vector, ALL)]
    unnamed x146 -> x135, local copies, waits for them, and re-layouts: 7.14 us -> 28.3 us
    select_n x28 -> x1, other arithmetic: 20.5 us -> 1.05 us  [per_device(): jnp.where(x == 3, chip[1, :, 128:], tail)]
    dot_general x11 -> x7, matrix products: 27.3 us -> 9.96 us  [the longest x1 3.88 us: per_device(): jnp.einsum('koi,ti->kot', weight_qkv, flat_rows, preferred_element_type=F32)]
    convert_element_type x20 -> x1, other arithmetic: 12.2 us -> 0.31 us  [per_device(): in_grad = parted((d_residual + part).astype(BF))]
  transfers between devices with their start and end apart: 66 -> 0, of which waited for: 23 -> 0; matrix products, arithmetic and copies ran while one was open for 14% -> 0% of each run, Pallas kernels for 10% -> 0%
where the time goes in v2:
time: 345 us; the launch traced here: 338 us
  Pallas kernels  263 us (76%)
  local copies, waits for them, and re-layouts  46.1 us (13%)
  matrix products  13.6 us (4%)
  other arithmetic  13.5 us (4%)
    pallas_call x8, Pallas kernels, call(): pl.pallas_call(kernel, out_shape=tuple((jax.ShapeDtypeStruct(shape, dtype...  246 us
    unnamed x135, local copies, waits for them, and re-layouts  28.3 us
    pallas_call x1, Pallas kernels, hidden_part(): pl.pallas_call(hidden_kernel, grid=(LEN // BLOCK,), in_specs=[rows, rows,...  16.4 us

profile of v2, /device:TPU:6, one launch (start us, length us, event | category | flops | bytes accessed | tf_op | source)
XLA Modules:
  0.0 338.1 jit_solution(4518384889505221755)
XLA Ops:
  0.7 1.2 copy.37.a_ref
  7.0 14.2 %enter.1 = (bf16[2,128,544]{2,1,0:T(8,128)(2,1)S(1)}, bf16[4,136,544]{2,1,0:T(8,128)(2,1)S(1)}, f32[2,8,544]{2,1,0:T(8,128)S(1)}) custom-call(bf16[2,128,544]{2,1,0:T(8,128)(2,1)S(1)} %copy.37.a_ref, bf16[136,544]{1,0:T(8,128)(2,1)S(1)} %copy-done.27, f32[8,544]{1,0:T(8,128)S(1)} %stack.75.cols_ref), custom_call_target="tpu_custom_call" | custom-call | tf_op jit(solution)/shard_map/enter/pallas_call | solution.py:113
  22.3 33.7 %first.1 = (bf16[8,128,1088]{2,1,0:T(8,128)(2,1)S(1)}, bf16[2,128,544]{2,1,0:T(8,128)(2,1)S(1)}, bf16[2,2,3,136,544]{4,3,2,1,0:T(8,128)(2,1)S(1)}, bf16[2,3,48,5...) custom-call(bf16[128,1088]{1,0:T(8,128)(2,1)S(1)} %fusion.19.n_ref, ...), custom_call_target="tpu_custom_call" | custom-call | tf_op jit(solution)/shard_map/first/pallas_call | solution.py:113
  56.2 1.4 copy-done.1
  58.4 2.0 fusion.12
  61.2 3.9 %add_convert_fusion.qkv_ref = bf16[3,192,1024]{2,1,0:T(8,128)(2,1)S(1)} fusion(bf16[1024,1088,1]{1,0,2:T(8,128)(2,1)} %bitcast.110, f32[3,192]{1,0:T(4,128)S(1)} %pad_maximum_fusion.9, bf16[3,192,544]{2,1,0:T(8,128)(2,1)} %get-tuple-element.172, bf16[3,192,544]{2,1,0:T(8,128)(2,1)} %get-tuple-element.171, pred[192]{0:T(512)(128)(4,1)S(1)} %compare_or_fusion), kind=kOutput, calls=%fused_computation.7 | convolution fusion | flops 1287770112 | bytes 4663744 | tf_op jit(solution)/shard_map/koi,ti->kot/dot_general | solution.py:768
  65.9 25.1 %attend.1 = (bf16[192,1024]{1,0:T(8,128)(2,1)S(1)}, bf16[3,1024,1024]{2,1,0:T(8,128)(2,1)}, bf16[8,192,128]{2,1,0:T(8,128)(2,1)S(1)}, bf16[8,128,1088]{2,1,0:T(8,128)(2,1)S(1)}) custom-call(bf16[3,192,1024]{2,1,0:T(8,128)(2,1)S(1)} %add_convert_fusion.qkv_ref, bf16[128,1088]{1,0:T(8,128)(2,1)S(1)} %get-tuple-element.139.t_ref), custom_call_target="tpu_custom_call" | custom-call | tf_op jit(solution)/shard_map/attend/pallas_call | solution.py:113
  91.4 1.2 copy-done.6
  95.8 27.9 %second.1 = (bf16[8,128,1088]{2,1,0:T(8,128)(2,1)S(1)}, bf16[2,4,136,544]{3,2,1,0:T(8,128)(2,1)S(1)}, bf16[2,4,136,544]{3,2,1,0:T(8,128)(2,1)S(1)}) custom-call(bf16[128,1088]{1,0:T(8,128)(2,1)S(1)} %add_convert_fusion.1.n_ref, bf16[4,136,544]{2,1,0:T(8,128)(2,1)S(1)} %bitcast.106, bf16[4,136,544]{2,1,0:T(8,128)(2,1)S(1)} %bitcast.107), custom_call_target="tpu_custom_call" | custom-call | tf_op jit(solution)/shard_map/second/pallas_call | solution.py:113
  123.8 1.4 copy-done.7
  125.2 1.1 copy-done.9
  126.4 1.3 copy-done.10
  127.7 16.4 %hidden_part.1 = (bf16[8,128,1088]{2,1,0:T(8,128)(2,1)S(1)}, bf16[8,128,1088]{2,1,0:T(8,128)(2,1)}, bf16[2,8,68,544]{3,2,1,0:T(8,128)(2,1)S(1)}, bf16[2,8,68,544]{3,2,1,0:T(8,128)(2,1)S(1)}, f32[1,544]{1,0:T(1,128)S(1)}) custom-call(bf16[8,128,1088]{2,1,0:T(8,128)(2,1)} %copy-done.7, bf16[8,128,1088]{2,1,0:T(8,128)(2,1)} %copy-done.6, ...), custom_call_target="tpu_custom_call" | custom-call | tf_op jit(solution)/shard_map/hidden_part/pallas_call | solution.py:478
  144.2 1.5 copy-done.3
  145.6 1.7 copy-done.5
  147.3 32.5 %third.1 = (f32[128,1088]{1,0:T(8,128)S(1)}, bf16[68,544]{1,0:T(8,128)(2,1)S(1)}) custom-call(bf16[8,128,1088]{2,1,0:T(8,128)(2,1)S(1)} %copy-done.5, bf16[2,8,68,544]{3,2,1,0:T(8,128)(2,1)S(1)} %get-tuple-element.65.g_ref), custom_call_target="tpu_custom_call" | custom-call | tf_op jit(solution)/shard_map/third/pallas_call | solution.py:113
  180.6 1.7 convert_reduce_fusion.3
  184.2 34.0 %back.1 = (bf16[3,192,1024]{2,1,0:T(8,128)(2,1)S(1)}, bf16[8,128,1088]{2,1,0:T(8,128)(2,1)S(1)}, bf16[68,544]{1,0:T(8,128)(2,1)S(1)}) custom-call(bf16[1088,128]{1,0:T(8,128)(2,1)S(1)} %fusion.1.m_ref, bf16[128,1088]{1,0:T(8,128)(2,1)S(1)} %get-tuple-element.141.a_ref, bf16[3,192,1024]{2,1,0:T(8,128)(2,1)S(1)} %add_convert_fusion.qkv_ref, ...), custom_call_target="tpu_custom_call" | custom-call | tf_op jit(solution)/shard_map/back/pallas_call | solution.py:113
  221.3 3.4 convolution_convert_fusion
  225.2 1.6 pad_maximum_fusion.s_ref
  226.8 3.7 %bitcast_convert_fusion = bf16[1024,1088]{0,1:T(8,128)(2,1)} fusion(bf16[3,192,1024]{2,1,0:T(8,128)(2,1)S(1)} %copy-done.14, bf16[3,192,544]{2,1,0:T(8,128)(2,1)S(1)} %copy-done.47, bf16[3,192,544]{2,1,0:T(8,128)(2,1)S(1)} %copy-done.46, pred[192]{0:T(512)(128)(4,1)S(1)} %copy-done.61), kind=kOutput, calls=%fused_computation | convolution fusion | flops 1287704576 | bytes 4661440 | tf_op jit(solution)/shard_map/kot,koi->ti/dot_general | solution.py:800
  230.4 3.0 copy.44
  233.5 1.5 copy-done
  235.0 27.4 %fourth.1 = (f32[128,1088]{1,0:T(8,128)S(1)}, bf16[8,68,544]{2,1,0:T(8,128)(2,1)S(1)}, bf16[8,68,544]{2,1,0:T(8,128)(2,1)S(1)}, bf16[2,4,192,544]{3,2,1,0:T(8,128)(2,1)S(1)}, bf16[4,48,544]{2,1,0:T(8,128)(2,1)S(1)}) custom-call(bf16[8,128,1088]{2,1,0:T(8,128)(2,1)S(1)} %bitcast.100, bf16[68,544]{1,0:T(8,128)(2,1)S(1)} %copy-done.31, ...), custom_call_target="tpu_custom_call" | custom-call | tf_op jit(solution)/shard_map/fourth/pallas_call | solution.py:113
  262.4 1.3 copy-done.11
  267.8 1.2 slice_bitcast_fusion
  269.0 2.0 fusion.3
  273.8 1.7 copy-done.4
  276.3 51.5 %leave.1 = (bf16[2,128,544]{2,1,0:T(8,128)(2,1)S(1)}, bf16[2,128,544]{2,1,0:T(8,128)(2,1)S(1)}, bf16[8,68,544]{2,1,0:T(8,128)(2,1)S(1)}, f32[8,24,128]{2,1,0:T(8,128)S(1)}) custom-call(bf16[8,128,1088]{2,1,0:T(8,128)(2,1)S(1)} %copy-done.4, f32[128,1088]{1,0:T(8,128)S(1)} %copy-done.8, bf16[2,128,544]{2,1,0:T(8,128)(2,1)S(1)} %pad_maximum_fusion.2.i_ref, ...), custom_call_target="tpu_custom_call" | custom-call | tf_op jit(solution)/shard_map/leave/pallas_call | solution.py:113
  329.3 1.1 slice.184
  335.1 1.3 reshape.189
  336.4 1.3 reshape.190
  (210 shorter events, 32.0 us)
Async XLA Ops:
  0.6 21.2 %copy-start.48 = (bf16[2,128,544]{1,2,0:T(8,128)(2,1)S(1)}, bf16[2,128,544]{1,2,0:T(8,128)(2,1)}, u32[]{:S(2)}) copy-start(bf16[2,128,544]{1,2,0:T(8,128)(2,1)} %param.27) | copy-start | bytes 835588
  7.0 15.1 %copy-start.15 = (bf16[3,136,544]{2,1,0:T(8,128)(2,1)S(1)}, bf16[3,136,544]{2,1,0:T(8,128)(2,1)}, u32[]{:S(2)}) copy-start(bf16[3,136,544]{2,1,0:T(8,128)(2,1)} %w_ref.1) | copy-start | bytes 1331716
  21.3 73.0 %copy-start.39 = (bf16[128,544]{1,0:T(8,128)(2,1)}, bf16[128,544]{1,0:T(8,128)(2,1)S(1)}, u32[]{:S(2)}) copy-start(bf16[128,544]{1,0:T(8,128)(2,1)S(1)} %get-tuple-element.159) | copy-start | bytes 417796
  21.3 73.0 %copy-start.42 = (bf16[128,544]{1,0:T(8,128)(2,1)}, bf16[128,544]{1,0:T(8,128)(2,1)S(1)}, u32[]{:S(2)}) copy-start(bf16[128,544]{1,0:T(8,128)(2,1)S(1)} %get-tuple-element.160) | copy-start | bytes 417796
  21.5 34.5 %copy-start.55 = (f32[128]{0:T(128)}, f32[128]{0:T(128)S(1)}, u32[]{:S(2)}) copy-start(f32[128]{0:T(128)S(1)} %get-tuple-element.174) | copy-start | bytes 1540
  56.0 1.6 copy-start.1
  56.0 2.4 copy-start.34
  61.0 4.1 %copy-start.59 = (pred[192]{0:T(512)(128)(4,1)}, pred[192]{0:T(512)(128)(4,1)S(1)}, u32[]{:S(2)}) copy-start(pred[192]{0:T(512)(128)(4,1)S(1)} %compare_or_fusion) | copy-start | bytes 580
  65.1 26.0 %copy-start.2 = (bf16[2,2,4,136,544]{4,3,2,1,0:T(8,128)(2,1)S(1)}, bf16[2,2,4,136,544]{4,3,2,1,0:T(8,128)(2,1)}, u32[]{:S(2)}) copy-start(bf16[2,2,4,136,544]{4,3,2,1,0:T(8,128)(2,1)} %copy-done.1) | copy-start | bytes 7102468
  145.6 1.7 copy-start.5
  179.8 2.5 copy-start.28
  180.6 1.7 copy-start.36
  184.2 35.3 %copy-start.60 = (pred[192]{0:T(512)(128)(4,1)S(1)}, pred[192]{0:T(512)(128)(4,1)}, u32[]{:S(2)}) copy-start(pred[192]{0:T(512)(128)(4,1)} %copy-done.59) | copy-start | bytes 580
  218.3 1.7 copy-start.23
  225.1 1.6 copy-start.46
  225.2 1.6 copy-start.47
  230.4 3.0 copy-start.29
  230.4 3.0 copy-start.31
  235.0 30.5 %copy-start.40 = (bf16[128,544]{1,0:T(8,128)(2,1)S(1)}, bf16[128,544]{1,0:T(8,128)(2,1)}, u32[]{:S(2)}) copy-start(bf16[128,544]{1,0:T(8,128)(2,1)} %copy-done.39) | copy-start | bytes 417796
  235.0 30.5 %copy-start.43 = (bf16[128,544]{1,0:T(8,128)(2,1)S(1)}, bf16[128,544]{1,0:T(8,128)(2,1)}, u32[]{:S(2)}) copy-start(bf16[128,544]{1,0:T(8,128)(2,1)} %copy-done.42) | copy-start | bytes 417796
  235.0 30.5 %copy-start.56 = (f32[128]{0:T(128)S(1)}, f32[128]{0:T(128)}, u32[]{:S(2)}) copy-start(f32[128]{0:T(128)} %copy-done.55) | copy-start | bytes 1540
  235.0 30.9 %copy-start.54 = (f32[1088]{0:T(1024)S(1)}, f32[1088]{0:T(1024)}, u32[]{:S(2)}) copy-start(f32[1088]{0:T(1024)} %get-tuple-element.140) | copy-start | bytes 13060
  235.0 30.9 %copy-start.53 = (f32[1088]{0:T(1024)S(1)}, f32[1088]{0:T(1024)}, u32[]{:S(2)}) copy-start(f32[1088]{0:T(1024)} %get-tuple-element.112) | copy-start | bytes 13060
  235.0 31.0 %copy-start.52 = (f32[1088]{0:T(1024)S(1)}, f32[1088]{0:T(1024)}, u32[]{:S(2)}) copy-start(f32[1088]{0:T(1024)} %get-tuple-element.118) | copy-start | bytes 13060
  235.0 31.0 %copy-start.51 = (f32[1088]{0:T(1024)S(1)}, f32[1088]{0:T(1024)}, u32[]{:S(2)}) copy-start(f32[1088]{0:T(1024)} %get-tuple-element.138) | copy-start | bytes 13060
  235.0 31.0 %copy-start.50 = (f32[2,1088]{1,0:T(2,128)S(1)}, f32[2,1088]{1,0:T(2,128)}, u32[]{:S(2)}) copy-start(f32[2,1088]{1,0:T(2,128)} %copy-done.49) | copy-start | bytes 26116
  265.5 2.3 copy-start.12
  273.8 1.7 copy-start.4
  330.4 1.8 copy-start.25
  330.4 2.7 copy-start.33
  330.4 4.7 %copy-start.19 = (bf16[8,68,544]{2,1,0:T(8,128)(2,1)S(1)}, bf16[8,68,544]{2,1,0:T(8,128)(2,1)}, u32[]{:S(2)}) copy-start(bf16[8,68,544]{2,1,0:T(8,128)(2,1)} %copy-done.18) | copy-start | bytes 1775620
  332.2 4.2 %copy-start.17 = (bf16[8,68,544]{2,1,0:T(8,128)(2,1)S(1)}, bf16[8,68,544]{2,1,0:T(8,128)(2,1)}, u32[]{:S(2)}) copy-start(bf16[8,68,544]{2,1,0:T(8,128)(2,1)} %copy-done.16) | copy-start | bytes 1775620
  (31 other events, 36.1 us)
